TPU v7x, 256 devices: a whole 4x4x8 slice. The times are simulated.
256 devices in a mesh: dp: 4 (over z_hi, core), tensor: 64 (over y, x, z_lo).
Axes of the slice: x: 4, y: 4, z: 8 (z_hi: 2, z_lo: 4; z = z_hi * 4 + z_lo), core: 2. Of those that a mesh axis runs over, the one named last changes fastest.
Arguments:
- hidden: bfloat16 [1024, 28672], P('dp', 'tensor'), may hold values from -6 to 6
- weight: bfloat16 [28672, 8192], P('tensor'), may hold values from -0.09375 to 0.09375
- factors: bfloat16 [6, 448, 64, 64], P(None, 'tensor'), may hold values from -0.29882812 to 0.29882812
- cotangent: bfloat16 [1024, 8192], P('dp', 'tensor'), may hold values from -6 to 6
Outputs:
- projected: bfloat16 [1024, 8192], P('dp', 'tensor')
- hidden_grad: bfloat16 [1024, 28672], P('dp', 'tensor')
- factor_grad: float32 [6, 448, 64, 64], P(None, 'tensor')
All inputs are finite; a program needn't handle non-finite values.
Results may differ from a plain program's by a relative error of at most 0.02.
Values may be sent and summed in bfloat16 or wider, within the bound.
A program may use at most 128 MiB of HBM per device.

v0:
```python
import jax
import jax.numpy as jnp
from jax import lax
from jax.sharding import PartitionSpec as P

LANES = 7


def partner_2(array, axis, stride):
    return lax.ppermute(array, axis, [(i, i ^ 1 << stride) for i in range(lax.axis_size(axis))])


def pair_inputs(own_part, partner, is_upper):
    side_mask = is_upper[None, :, None, None]
    lower_x = jnp.where(side_mask, partner, own_part)
    upper_x = jnp.where(side_mask, own_part, partner)
    dims_of = own_part.shape
    split_shape = dims_of[:3] + (2, dims_of[3] // 2)
    return jnp.concatenate([lower_x.reshape(split_shape), upper_x.reshape(split_shape)], axis=4)


def body(hidden, weight, factors, cotangent):
    tokens_here, width_here = hidden.shape
    sections, blocks_here, block_size, unused_dim = factors.shape
    half_width = block_size // 2
    groups_here = blocks_here // LANES
    local_levels = groups_here.bit_length() - 1
    first_group = lax.axis_index("tensor") * groups_here

    def upper_of(section_no):
        group_ids = first_group + jnp.arange(groups_here, dtype=jnp.int32)
        return group_ids >> section_no & 1 == 1

    def factor_of(section_no):
        return factors[section_no].reshape(groups_here, LANES, block_size, block_size)

    current = hidden.reshape(tokens_here, groups_here, LANES, block_size)
    stored = []
    for section_no in range(sections):
        partner = partner_2(current, "tensor", section_no - local_levels)
        mixed_in = pair_inputs(current, partner, upper_of(section_no))
        fac_r = factor_of(section_no).reshape(groups_here, LANES, block_size, 2, half_width)
        mix_term = jnp.einsum(
            "tqjhm,qjmhk->tqjhk", mixed_in, fac_r, preferred_element_type=jnp.float32
        )
        stored.append(mixed_in)
        current = (current.astype(jnp.float32) + mix_term.reshape(current.shape)).astype(
            jnp.bfloat16
        )
    rotated = current.reshape(tokens_here, width_here)
    columns = weight
    summed = lax.psum_scatter(
        lax.dot_general(
            columns, rotated, (((0,), (1,)), ((), ())), preferred_element_type=jnp.float32
        ),
        "tensor",
        scatter_dimension=0,
        tiled=True,
    )
    projected = summed.T.astype(jnp.bfloat16)
    columns = weight
    pulled = lax.dot_general(
        lax.all_gather(cotangent, "tensor", axis=1, tiled=True),
        columns,
        (((1,), (1,)), ((), ())),
        preferred_element_type=jnp.float32,
    )
    grad_now = pulled.astype(jnp.bfloat16).reshape(current.shape)
    count_all = tokens_here * lax.axis_size("dp")
    split_shape = current.shape[:3] + (2, half_width)
    factor_parts = [None] * sections
    for section_no in reversed(range(sections)):
        block_fac = factor_of(section_no)
        is_upper = upper_of(section_no)
        swap_bit = section_no - local_levels
        partner_grad, partner_fac = partner_2((grad_now, block_fac), "tensor", swap_bit)
        mixed_in = stored[section_no]
        own_grad = grad_now.reshape(split_shape)
        fac_r = block_fac.reshape(groups_here, LANES, block_size, 2, half_width)
        partner_r = partner_fac.reshape(groups_here, LANES, block_size, 2, half_width)
        local_grad = jnp.einsum(
            "tqjhm,tqjhk->qjmhk", mixed_in, own_grad, preferred_element_type=jnp.float32
        )
        local_grad = local_grad.reshape(blocks_here, block_size, block_size)
        spread = jnp.einsum(
            "tqjhk,qjmhk->tqjhm", own_grad, fac_r, preferred_element_type=jnp.float32
        )
        spread = spread + jnp.einsum(
            "tqjhk,qjmhk->tqjhm",
            partner_grad.reshape(split_shape),
            partner_r,
            preferred_element_type=jnp.float32,
        )
        own_part = jnp.where(
            is_upper[None, :, None, None, None], spread[..., half_width:], spread[..., :half_width]
        )
        grad_now = (
            (own_grad.astype(jnp.float32) + own_part).astype(jnp.bfloat16).reshape(current.shape)
        )
        factor_parts[section_no] = lax.psum(local_grad, "dp")
    stacked = jnp.stack(factor_parts)
    factor_grad = stacked / jnp.float32(count_all)
    return (projected, grad_now.reshape(tokens_here, width_here), factor_grad)


def solution(mesh):
    placed = (
        P("dp", "tensor"),
        P("tensor", None),
        P(None, "tensor", None, None),
        P("dp", "tensor"),
    )
    return jax.shard_map(
        body,
        mesh=mesh,
        in_specs=placed,
        out_specs=(P("dp", "tensor"), P("dp", "tensor"), P(None, "tensor", None, None)),
        check_vma=False,
    )
```

profile of v0, /device:TPU:0, one launch (start us, length us, event | category | flops | bytes accessed | tf_op | source)
XLA Modules:
  0.0 863.9 jit_solution(13742910825147646428)
XLA Ops:
  8.2 1.9 fusion.68
  10.8 3.4 collective-permute-done
  14.6 3.1 collective-permute-start.1
  18.8 10.2 %collective-permute-done.1 = bf16[256,1,7,64]{0,3,2,1:T(8,128)(2,1)S(1)} collective-permute-done((bf16[256,1,7,64]{0,3,2,1:T(8,128)(2,1)S(1)}, bf16[256,1,7,64]{0,3,2,1:T(8,128)(2,1)S(1)}, u32[]{:S(2)}, u32[]{:S(2)}) %collective-permute-start.1) | collective-permute-done | bytes 229408 | tf_op jit(solution)/shard_map/ppermute | solution.py:10
  31.9 4.3 collective-permute-done.2
  36.5 2.8 collective-permute-start.3
  39.5 6.2 collective-permute-done.3
  46.0 1.8 collective-permute-start.4
  48.8 3.4 collective-permute-done.4
  52.5 4.8 collective-permute-start.5
  57.3 2.0 collective-permute-start.11
  59.5 4.5 collective-permute-done.11
  64.6 1.8 collective-permute-start.9
  67.5 1.7 copy.15
  69.2 1.7 copy.16
  74.9 239.0 %all-gather.2.cloned.1.call-done = bf16[256,8192]{1,0:T(8,128)(2,1)} async-done(((bf16[256,128]{1,0:T(8,128)(2,1)}), bf16[256,8192]{1,0:T(8,128)(2,1)}) %all-gather.2.cloned.1.call-update) | async-done | bytes 4194320 | tf_op jit(solution)/shard_map/all_gather | solution.py:63
  313.9 6.5 convolution_convert_fusion
  321.7 1.8 copy.24
  323.8 4.6 collective-permute-done.6
  331.8 1.7 copy.23
  333.9 5.7 collective-permute-done.8
  341.5 1.7 copy.22
  343.6 7.2 collective-permute-done.10
  352.8 1.8 copy.21
  354.9 5.7 collective-permute-done.12
  362.6 1.8 copy.20
  364.7 6.8 collective-permute-done.14
  373.9 8.8 %convolution_bitcast_fusion = f32[8192,256]{0,1:T(8,128)} fusion(bf16[256,448]{0,1:T(8,128)(2,1)S(1)} %fusion.18, bf16[448,8192]{1,0:T(8,128)(2,1)} %param.5), kind=kOutput, calls=%fused_computation | convolution fusion | flops 1879048192 | bytes 15958016 | tf_op jit(solution)/shard_map/dot_general | solution.py:53
  383.6 7.8 collective-permute-done.17
  392.0 16.0 %collective-permute-done.16 = bf16[256,1,7,64]{0,3,2,1:T(8,128)(2,1)S(1)} collective-permute-done((bf16[256,1,7,64]{0,3,2,1:T(8,128)(2,1)S(1)}, bf16[256,1,7,64]{0,3,2,1:T(8,128)(2,1)S(1)}, u32[]{:S(2)}, u32[]{:S(2)}) %collective-permute-start.16) | collective-permute-done | bytes 229408 | tf_op jit(solution)/shard_map/ppermute | solution.py:10
  409.2 44.5 %all-reduce.3.cloned.1.call-done = (f32[1,7,64,64]{3,2,1,0:T(8,128)}, f32[1,7,64,64]{3,2,1,0:T(8,128)}, f32[1,7,64,64]{3,2,1,0:T(8,128)}, f32[1,7,64,64]{3,2,1,0...) async-done(((f32[1,7,64,64]{3,2,1,0:T(8,128)}, f32[1,7,64,64]{3,2,1,0:T(8,128)}, f32[1,7,64,64]{3,2,1,0:T(8,128)}, f32[1,7,64,64]{3,2,1,0:T(8,128)}, ...) | async-done | bytes 688144 | tf_op jit(solution)/shard_map/psum | solution.py:100
  458.0 397.9 %reduce-scatter.2.cloned.1.call-done = f32[128,256]{0,1:T(8,128)} async-done(((f32[8192,256]{0,1:T(8,128)}), f32[128,256]{0,1:T(8,128)}) %reduce-scatter.2.cloned.1.call-update) | async-done | bytes 131088 | tf_op jit(solution)/shard_map/reduce_scatter | solution.py:52
  (172 shorter events, 36.6 us)
Async XLA Ops:
  7.2 306.8 %all-gather.2.cloned.1.call-start = ((), (), s32[]{:S(2)}) async-start(), calls=%async_computation.2 | async-start | bytes 4259840 | tf_op jit(solution)/shard_map/all_gather | solution.py:63
  7.9 445.8 %all-reduce.3.cloned.1.call-start = ((), (), s32[]{:S(2)}) async-start(), calls=%async_computation.3 | async-start | bytes 2752512 | tf_op jit(solution)/shard_map/psum | solution.py:100
  8.0 6.3 collective-permute-start
  10.2 29.2 %copy-start.35 = (bf16[1,7,64,64]{3,2,1,0:T(8,128)(2,1)}, bf16[1,7,64,64]{3,2,1,0:T(8,128)(2,1)S(1)}, u32[]{:S(2)}) copy-start(bf16[1,7,64,64]{3,2,1,0:T(8,128)(2,1)S(1)} %get-tuple-element.10) | copy-start | bytes 172036
  14.3 14.7 %copy-start.10 = (bf16[256,1,7,64]{0,3,2,1:T(8,128)(2,1)}, bf16[256,1,7,64]{0,3,2,1:T(8,128)(2,1)S(1)}, u32[]{:S(2)}) copy-start(bf16[256,1,7,64]{0,3,2,1:T(8,128)(2,1)S(1)} %get-tuple-element.26) | copy-start | bytes 688132
  14.6 14.4 %collective-permute-start.1 = (bf16[256,1,7,64]{0,3,2,1:T(8,128)(2,1)S(1)}, bf16[256,1,7,64]{0,3,2,1:T(8,128)(2,1)S(1)}, u32[]{:S(2)}, u32[]{:S(2)}) collective-permute-start(bf16[256,1,7,64]{0,3,2,1:T(8,128)(2,1)S(1)} %fusion.27), channel_id=1, source_target_pairs={{0,2},{1,3},{2,0},{3,1},{4,6},{5,7},{6,4},{7,5},{8,10},{9,11},{10,... | collective-permute-start | bytes 688136 | tf_op jit(solution)/shard_map/ppermute | solution.py:10
  18.7 10.6 %copy-start.1 = (bf16[1,7,64,64]{2,3,1,0:T(8,128)(2,1)}, bf16[1,7,64,64]{2,3,1,0:T(8,128)(2,1)S(1)}, u32[]{:S(2)}) copy-start(bf16[1,7,64,64]{2,3,1,0:T(8,128)(2,1)S(1)} %copy.8) | copy-start | bytes 172036
  29.3 6.9 collective-permute-start.2
  36.2 9.5 %copy-start.16 = (bf16[256,1,7,64]{0,3,2,1:T(8,128)(2,1)}, bf16[256,1,7,64]{0,3,2,1:T(8,128)(2,1)S(1)}, u32[]{:S(2)}) copy-start(bf16[256,1,7,64]{0,3,2,1:T(8,128)(2,1)S(1)} %get-tuple-element.21) | copy-start | bytes 688132
  36.2 9.5 %copy-start.18 = (bf16[256,1,7,64]{0,3,2,1:T(8,128)(2,1)}, bf16[256,1,7,64]{0,3,2,1:T(8,128)(2,1)S(1)}, u32[]{:S(2)}) copy-start(bf16[256,1,7,64]{0,3,2,1:T(8,128)(2,1)S(1)} %get-tuple-element.22) | copy-start | bytes 688132
  36.5 9.1 %collective-permute-start.3 = (bf16[256,1,7,64]{0,3,2,1:T(8,128)(2,1)S(1)}, bf16[256,1,7,64]{0,3,2,1:T(8,128)(2,1)S(1)}, u32[]{:S(2)}, u32[]{:S(2)}) collective-permute-start(bf16[256,1,7,64]{0,3,2,1:T(8,128)(2,1)S(1)} %fusion.23), channel_id=1, source_target_pairs={{0,8},{1,9},{2,10},{3,11},{4,12},{5,13},{6,14},{7,15},{8,0},{9,1},... | collective-permute-start | bytes 688136 | tf_op jit(solution)/shard_map/ppermute | solution.py:10
  46.0 6.2 collective-permute-start.4
  52.2 11.7 %copy-start.24 = (bf16[256,1,7,64]{0,3,2,1:T(8,128)(2,1)}, bf16[256,1,7,64]{0,3,2,1:T(8,128)(2,1)S(1)}, u32[]{:S(2)}) copy-start(bf16[256,1,7,64]{0,3,2,1:T(8,128)(2,1)S(1)} %get-tuple-element.17) | copy-start | bytes 688132
  52.3 11.7 %copy-start.26 = (bf16[256,1,7,64]{0,3,2,1:T(8,128)(2,1)}, bf16[256,1,7,64]{0,3,2,1:T(8,128)(2,1)S(1)}, u32[]{:S(2)}) copy-start(bf16[256,1,7,64]{0,3,2,1:T(8,128)(2,1)S(1)} %get-tuple-element.18) | copy-start | bytes 688132
  52.5 21.4 %collective-permute-start.5 = (bf16[256,1,7,64]{0,3,2,1:T(8,128)(2,1)S(1)}, bf16[256,1,7,64]{0,3,2,1:T(8,128)(2,1)S(1)}, u32[]{:S(2)}, u32[]{:S(2)}) collective-permute-start(bf16[256,1,7,64]{0,3,2,1:T(8,128)(2,1)S(1)} %fusion.19), channel_id=1, source_target_pairs={{0,32},{1,33},{2,34},{3,35},{4,36},{5,37},{6,38},{7,39},{8,40},{9,... | collective-permute-start | bytes 688136 | tf_op jit(solution)/shard_map/ppermute | solution.py:10
  57.3 6.6 collective-permute-start.11
  59.4 9.8 %collective-permute-start.13 = (bf16[1,7,64,64]{3,2,1,0:T(8,128)(2,1)}, bf16[1,7,64,64]{3,2,1,0:T(8,128)(2,1)}, u32[]{:S(2)}, u32[]{:S(2)}) collective-permute-start(bf16[1,7,64,64]{3,2,1,0:T(8,128)(2,1)} %get-tuple-element.11), channel_id=1, source_target_pairs={{0,4},{1,5},{2,6},{3,7},{4,0},{5,1},{6,2},{7,3},{8,12},{9,13},{10,... | collective-permute-start | bytes 172040 | tf_op jit(solution)/shard_map/ppermute | solution.py:10
  59.4 11.4 %collective-permute-start.15 = (bf16[1,7,64,64]{3,2,1,0:T(8,128)(2,1)}, bf16[1,7,64,64]{3,2,1,0:T(8,128)(2,1)S(1)}, u32[]{:S(2)}, u32[]{:S(2)}) collective-permute-start(bf16[1,7,64,64]{3,2,1,0:T(8,128)(2,1)} %get-tuple-element.12), channel_id=1, source_target_pairs={{0,2},{1,3},{2,0},{3,1},{4,6},{5,7},{6,4},{7,5},{8,10},{9,11},{10,... | collective-permute-start | bytes 172040 | tf_op jit(solution)/shard_map/ppermute | solution.py:10
  59.4 12.2 %collective-permute-start.7 = (bf16[1,7,64,64]{3,2,1,0:T(8,128)(2,1)}, bf16[1,7,64,64]{3,2,1,0:T(8,128)(2,1)S(1)}, u32[]{:S(2)}, u32[]{:S(2)}) collective-permute-start(bf16[1,7,64,64]{3,2,1,0:T(8,128)(2,1)} %get-tuple-element.13), channel_id=1, source_target_pairs={{0,32},{1,33},{2,34},{3,35},{4,36},{5,37},{6,38},{7,39},{8,40},{9,... | collective-permute-start | bytes 172040 | tf_op jit(solution)/shard_map/ppermute | solution.py:10
  64.6 7.7 collective-permute-start.9
  320.4 9.3 %copy-start.7 = (bf16[256,448]{0,1:T(8,128)(2,1)}, bf16[256,448]{0,1:T(8,128)(2,1)S(1)}, u32[]{:S(2)}) copy-start(bf16[256,448]{0,1:T(8,128)(2,1)S(1)} %convolution_convert_fusion) | copy-start | bytes 688132
  320.4 7.9 collective-permute-start.6
  330.8 8.7 %copy-start.39 = (bf16[1,7,64,64]{2,3,1,0:T(8,128)(2,1)S(1)}, bf16[1,7,64,64]{2,3,1,0:T(8,128)(2,1)}, u32[]{:S(2)}) copy-start(bf16[1,7,64,64]{2,3,1,0:T(8,128)(2,1)} %copy.14) | copy-start | bytes 172036
  333.5 6.0 collective-permute-start.8
  340.6 10.2 %copy-start.38 = (bf16[1,7,64,64]{2,3,1,0:T(8,128)(2,1)S(1)}, bf16[1,7,64,64]{2,3,1,0:T(8,128)(2,1)}, u32[]{:S(2)}) copy-start(bf16[1,7,64,64]{2,3,1,0:T(8,128)(2,1)} %copy.15) | copy-start | bytes 172036
  343.3 7.5 collective-permute-start.10
  354.6 6.0 collective-permute-start.12
  361.6 9.9 %copy-start.34 = (bf16[1,7,64,64]{2,3,1,0:T(8,128)(2,1)S(1)}, bf16[1,7,64,64]{2,3,1,0:T(8,128)(2,1)}, u32[]{:S(2)}) copy-start(bf16[1,7,64,64]{2,3,1,0:T(8,128)(2,1)} %copy.17) | copy-start | bytes 172036
  364.4 7.1 collective-permute-start.14
  373.6 482.2 %reduce-scatter.2.cloned.1.call-start = ((), (), s32[]{:S(2)}) async-start(), calls=%async_computation.1 | async-start | bytes 8519680 | tf_op jit(solution)/shard_map/reduce_scatter | solution.py:52
  383.6 7.8 collective-permute-start.17
  391.5 16.5 %collective-permute-start.16 = (bf16[256,1,7,64]{0,3,2,1:T(8,128)(2,1)S(1)}, bf16[256,1,7,64]{0,3,2,1:T(8,128)(2,1)S(1)}, u32[]{:S(2)}, u32[]{:S(2)}) collective-permute-start(bf16[256,1,7,64]{0,3,2,1:T(8,128)(2,1)S(1)} %bitcast.308), channel_id=1, source_target_pairs={{0,1},{1,0},{2,3},{3,2},{4,5},{5,4},{6,7},{7,6},{8,9},{9,8},{10,11... | collective-permute-start | bytes 688136 | tf_op jit(solution)/shard_map/ppermute | solution.py:10
  (33 other events, 113.7 us)
Sparse Core Ops, SparseCore 0:
  9.7 304.1 all-gather.1
  373.8 79.9 all-reduce.2
  456.4 399.4 reduce-scatter.1
where the time goes:
time: 865 us; the launch traced here: 864 us
  waiting for transfers between devices  768 us (89%)
  local copies, waits for them, and re-layouts  30.7 us (4%)
  matrix products  26.4 us (3%)
  starting transfers between devices  18.9 us (2%)
  between operations  14.4 us (2%)
    reduce_scatter x1, waiting for transfers between devices, body(): lax.psum_scatter(lax.dot_general(columns, rotated, (((0,), (1,)), ((), ()...  398 us
    all_gather x1, waiting for transfers between devices, body(): lax.all_gather(cotangent, 'tensor', axis=1, tiled=True)  239 us
    ppermute x18, waiting for transfers between devices, partner_2(): lax.ppermute(array, axis, [(i, i ^ 1 << stride) for i in range(lax.axis_s...  85.7 us
    psum x1, waiting for transfers between devices, body(): factor_parts[section_no] = lax.psum(local_grad, 'dp')  44.5 us
    ppermute x18, starting transfers between devices, partner_2(): lax.ppermute(array, axis, [(i, i ^ 1 << stride) for i in range(lax.axis_s...  18.8 us
  transfers between devices with their start and end apart: 21, of which 16 were waited for; matrix products, arithmetic and copies ran while one was open for 4% of the time, Pallas kernels for 0%

commit v1 on v0

v1 whole, which is shorter than its diff:
```python
import jax
import jax.numpy as jnp
from jax import lax
from jax.experimental import pallas as pl
from jax.experimental.pallas import tpu as pltpu
from jax.sharding import PartitionSpec as P

MESH = pl.DeviceIdType.MESH
BF16 = jnp.bfloat16
F32 = jnp.float32

ROWS = 256
WIDTH = 448
HALF = 32
SECTIONS = 6
SIDE = 4
COL = 128
BLOCK = SIDE * COL
CHUNK = 128
QUART = 64
TILES = ((0, 128), (128, 128), (256, 128), (384, 64))

SCHEDULE = (
    "G FA FB S FA FB G FA G FB G FA FB G FA FB G FA FB G BA BB FA FB D5 R "
    "BA BB D4 D5 R BA BB D3 D4 D5 R BA BB D2 D3 D4 D5 R BA BB D1 D2 D3 D4 R "
    "BA BB D0 D1 D2 D3 R BA BB D0 D1 D2 D0 D1 D0"
)


def dot(a, b, contract):
    return lax.dot_general(a, b, (contract, ((), ())), preferred_element_type=F32)


def kernel(
    hid, w_hbm, fac, cot, proj, hgrad, fgrad,
    wv, cotg, par, xs, xp, gs, gp, fac_t, fac_p, ma, mb, mp, fg, fg_core, fg_half, fg_far,
    fg_all, acc, ra1, ra2, rb1, rb2, sa1, sa2, sb1, sb2, zr, w_sem, send, recv,
):
    dp = lax.axis_index("dp")
    t = lax.axis_index("tensor")
    y = lax.div(t, SIDE * SIDE)
    x = lax.rem(lax.div(t, SIDE), SIDE)
    z = lax.rem(t, SIDE)

    def ring(v, k):
        return lax.rem(v + k, SIDE)

    def at(yy, xx, zz):
        return (dp, (yy * SIDE + xx) * SIDE + zz)

    def y_dev(k):
        return at(ring(y, k), x, z)

    def x_dev(k):
        return at(y, ring(x, k), z)

    def z_dev(k):
        return at(y, x, ring(z, k))

    core_dev = (dp + 1 - 2 * lax.rem(dp, 2), t)
    far_dev = (lax.rem(dp + 2, 4), t)

    def bit_of(s):
        return lax.rem(lax.div(t, 1 << s), 2)

    def partner(s):
        return (dp, t + (1 << s) * (1 - 2 * bit_of(s)))

    def own_rows(s):
        return pl.ds(pl.multiple_of(HALF * bit_of(s), HALF), HALF)

    def other_rows(s):
        return pl.ds(pl.multiple_of(HALF - HALF * bit_of(s), HALF), HALF)

    started = []

    def copy(src, dst, dev):
        k = len(started)
        c = pltpu.make_async_remote_copy(
            src_ref=src, dst_ref=dst, send_sem=send.at[k], recv_sem=recv.at[k],
            device_id=dev, device_id_type=MESH,
        )
        c.start()
        started.append(c)
        return c

    w_copies = []
    for b in range(SIDE * SIDE):
        c = pltpu.make_async_copy(w_hbm.at[:, pl.ds(b * BLOCK, BLOCK)], wv.at[b], w_sem.at[b])
        c.start()
        w_copies.append(c)

    peers = [f(k) for f in (z_dev, x_dev, y_dev) for k in (1, 2, 3)] + [core_dev, far_dev]
    barrier = pltpu.get_barrier_semaphore()
    for dev in peers:
        pl.semaphore_signal(barrier, inc=1, device_id=dev, device_id_type=MESH)
    pl.semaphore_wait(barrier, len(peers))

    rows_a = (pl.ds(0, QUART), pl.ds(QUART, QUART))
    rows_b = (pl.ds(CHUNK, QUART), pl.ds(CHUNK + QUART, QUART))
    chunks = (pl.ds(0, CHUNK), pl.ds(CHUNK, CHUNK))

    def gather_phase(view, i, dev):
        r1 = copy(view(i, 0), view(i, 0), dev(1))
        l2 = copy(view(i, 1), view(i, 1), dev(3))
        r2 = copy(view(i, 1), view(i, 1), dev(1))
        l1 = copy(view(i, 0), view(i, 0), dev(3))
        yield
        left, right = ring(i, 3), ring(i, 1)
        r1.wait_recv()
        far1 = copy(view(left, 0), view(left, 0), dev(1))
        l2.wait_recv()
        far2 = copy(view(right, 1), view(right, 1), dev(3))
        yield
        r2.wait_recv()
        l1.wait_recv()
        yield
        far1.wait_recv()
        far2.wait_recv()
        yield

    def grad_dots(n, place):
        def step(k, carry):
            yy, xx = place(k)
            acc[...] += dot(cotg[yy, xx], wv[yy * SIDE + xx], ((1,), (1,)))
            return carry

        lax.fori_loop(0, n, step, 0)

    def near(k):
        return ring(y, 3 + lax.div(k, 3)), ring(x, 3 + lax.rem(k, 3))

    def gather():
        mine = pl.ds(pl.multiple_of(z * COL, COL), COL)
        z_copies = [copy(cot, cotg.at[y, x, :, mine], z_dev(k)) for k in (1, 2, 3)]
        cotg[y, x, :, mine] = cot[...]
        acc[...] = jnp.zeros_like(acc)
        yield
        for c in z_copies:
            c.wait_recv()
        pa = gather_phase(lambda i, h: cotg.at[y, i, rows_a[h], :], x, x_dev)
        pb = gather_phase(lambda i, h: cotg.at[i, x, rows_b[h], :], y, y_dev)
        next(pa), next(pb)
        yield
        next(pa), next(pb)
        yield
        next(pa), next(pb)
        next(pa), next(pb)
        pa = gather_phase(lambda i, h: cotg.at[i, :, rows_a[h], :], y, y_dev)
        pb = gather_phase(lambda i, h: cotg.at[:, i, rows_b[h], :], x, x_dev)
        next(pa), next(pb)
        yield
        next(pa), next(pb)
        yield
        next(pa), next(pb)
        for c in w_copies:
            c.wait()
        grad_dots(9, near)
        yield
        next(pa), next(pb)
        grad_dots(
            7,
            lambda k: (
                ring(y, jnp.where(k < 4, 2, k - 1)),
                ring(x, jnp.where(k < 4, k, 2)),
            ),
        )
        gs[SECTIONS - 1] = acc[...].astype(BF16)
        yield

    diag = (
        lax.broadcasted_iota(jnp.int32, (COL, WIDTH), 0) // HALF
        == lax.rem(lax.broadcasted_iota(jnp.int32, (COL, WIDTH), 1), COL) // HALF
    )

    def spread(part):
        return jnp.where(diag, jnp.concatenate([part] * 4, axis=0), jnp.zeros((), BF16))

    fac_copies = [None] * SECTIONS

    def setup():
        for s in range(SECTIONS):
            fac_t[s] = jnp.concatenate([fac[s, j] for j in range(7)], axis=1)
        for s in reversed(range(SECTIONS)):
            fac_copies[s] = copy(fac_t.at[s, other_rows(s), :], fac_p.at[s], partner(s))
        for s in range(SECTIONS):
            ma[s] = spread(fac_t[s, own_rows(s), :])
            mb[s] = spread(fac_t[s, other_rows(s), :])
        yield

    def x_ref(s):
        return hid if s == 0 else xs.at[s - 1]

    def forward(rows):
        for s in range(SECTIONS):
            c = copy(x_ref(s).at[rows, :], xp.at[s, rows, :], partner(s))
            yield
            c.wait_recv()
            src, dst = x_ref(s), x_ref(s + 1)
            for lo, w in TILES:
                own = src[rows, lo : lo + w]
                mix = dot(own, ma[s, 0:w, lo : lo + w], ((1,), (0,)))
                mix += dot(xp[s, rows, lo : lo + w], mb[s, 0:w, lo : lo + w], ((1,), (0,)))
                dst[rows, lo : lo + w] = (own.astype(F32) + mix).astype(BF16)
        yield

    def proj_dots(n, place):
        def step(k, carry):
            yy, xx = place(k)
            out = dot(x_ref(SECTIONS)[...], wv[yy * SIDE + xx], ((1,), (0,)))
            par[yy, xx] = out.astype(BF16)
            return carry

        lax.fori_loop(0, n, step, 0)

    def add_to(ref, *others):
        total = ref[...].astype(F32)
        for o in others:
            total += o[...].astype(F32)
        ref[...] = total.astype(BF16)

    def scatter_phase(view, i, buf1, buf2, dev):
        p1, p2, m1 = ring(i, 1), ring(i, 2), ring(i, 3)
        a = copy(view(p2, 0), buf1.at[0], dev(1))
        b = copy(view(p2, 1), buf1.at[1], dev(3))
        yield
        c = copy(view(p1, 1), buf2.at[0, 1], dev(1))
        d = copy(view(m1, 0), buf2.at[1, 0], dev(3))
        yield
        a.wait_recv()
        add_to(view(p1, 0), buf1.at[0])
        e = copy(view(p1, 0), buf2.at[0, 0], dev(1))
        b.wait_recv()
        add_to(view(m1, 1), buf1.at[1])
        f = copy(view(m1, 1), buf2.at[1, 1], dev(3))
        yield
        c.wait_recv()
        f.wait_recv()
        add_to(view(i, 1), buf2.at[0, 1], buf2.at[1, 1])
        d.wait_recv()
        e.wait_recv()
        add_to(view(i, 0), buf2.at[0, 0], buf2.at[1, 0])
        yield

    def scatter():
        pa = scatter_phase(lambda i, h: par.at[i, :, rows_a[h], :], y, ra1, ra2, y_dev)
        pb = scatter_phase(lambda i, h: par.at[:, i, rows_b[h], :], x, rb1, rb2, x_dev)
        proj_dots(4, lambda k: (ring(y, 2), ring(x, k)))
        next(pa)
        proj_dots(3, lambda k: (ring(y, 3 + k), ring(x, 2)))
        next(pb)
        proj_dots(6, lambda k: (ring(y, 1 + 2 * lax.div(k, 3)), ring(x, 3 + lax.rem(k, 3))))
        next(pa)
        proj_dots(3, lambda k: (y, ring(x, 3 + k)))
        next(pb)
        yield
        next(pa), next(pb)
        yield
        next(pa), next(pb)
        pa = scatter_phase(lambda i, h: par.at[y, i, rows_a[h], :], x, sa1, sa2, x_dev)
        pb = scatter_phase(lambda i, h: par.at[i, x, rows_b[h], :], y, sb1, sb2, y_dev)
        next(pa), next(pb)
        next(pa), next(pb)
        yield
        next(pa), next(pb)
        yield
        next(pa), next(pb)

        def columns(zz):
            return pl.ds(pl.multiple_of(zz * COL, COL), COL)

        last = [
            [
                copy(par.at[y, x, chunks[h], columns(ring(z, k))], zr.at[h, k - 1], z_dev(k))
                for k in (1, 2, 3)
            ]
            for h in (0, 1)
        ]
        yield
        for h in (0, 1):
            total = par[y, x, chunks[h], columns(z)].astype(F32)
            for k in (1, 2, 3):
                last[h][k - 1].wait_recv()
                total += zr[h, k - 1].astype(F32)
            proj[chunks[h], :] = total.astype(BF16)
        yield

    def backward(rows, first):
        for s in reversed(range(SECTIONS)):
            c = copy(gs.at[s, rows, :], gp.at[s, rows, :], partner(s))
            if first:
                fac_copies[s].wait_recv()
                mp[s] = spread(fac_p[s])
            yield
            c.wait_recv()
            for lo, w in TILES:
                own = gs[s, rows, lo : lo + w]
                back = dot(own, ma[s, 0:w, lo : lo + w], ((1,), (1,)))
                back += dot(gp[s, rows, lo : lo + w], mp[s, 0:w, lo : lo + w], ((1,), (1,)))
                new = (own.astype(F32) + back).astype(BF16)
                if s == 0:
                    hgrad[rows, lo : lo + w] = new
                else:
                    gs[s - 1, rows, lo : lo + w] = new
        yield

    core = lax.rem(dp, 2)
    keep = pl.ds(pl.multiple_of(HALF * core, HALF), HALF)
    give = pl.ds(pl.multiple_of(HALF - HALF * core, HALF), HALF)

    def factor(s):
        for act, rows in ((x_ref(s), own_rows(s)), (xp.at[s], other_rows(s))):
            for lo, w in TILES:
                full = dot(act[:, lo : lo + w], gs[s, :, lo : lo + w], ((0,), (0,)))
                full = jnp.where(diag[:w, :w], full, 0.0)
                total = full[0:HALF]
                for g in range(1, w // HALF):
                    total += full[g * HALF : (g + 1) * HALF]
                fg[s, rows, lo : lo + w] = total
        a = copy(fg.at[s, give, :], fg_core.at[s], core_dev)
        yield
        a.wait_recv()
        fg_half[s] = (fg[s, keep, :] + fg_core[s]).astype(BF16)
        b = copy(fg_half.at[s], fg_far.at[s], far_dev)
        yield
        b.wait_recv()
        fg_all[s, keep, :] = fg_half[s].astype(F32) + fg_far[s].astype(F32)
        c = copy(fg_all.at[s, keep, :], fg_all.at[s, keep, :], core_dev)
        yield
        c.wait_recv()
        fgrad[s] = fg_all[s]
        yield

    chains = {
        "G": gather(),
        "S": setup(),
        "FA": forward(chunks[0]),
        "FB": forward(chunks[1]),
        "BA": backward(chunks[0], True),
        "BB": backward(chunks[1], False),
        "R": scatter(),
    }
    for s in range(SECTIONS):
        chains[f"D{s}"] = factor(s)
    for name in SCHEDULE.split():
        next(chains[name], None)
    for chain in chains.values():
        for _ in chain:
            pass
    assert len(started) == COPIES
    for c in started:
        c.wait_send()


COPIES = 105


def body(hidden, weight, factors, cotangent):
    vmem = pl.BlockSpec(memory_space=pltpu.VMEM)
    part = (SIDE, QUART, BLOCK)
    scratch = [
        ((SIDE * SIDE, WIDTH, BLOCK), BF16),
        ((SIDE, SIDE, ROWS, BLOCK), BF16),
        ((SIDE, SIDE, ROWS, BLOCK), BF16),
        ((SECTIONS, ROWS, WIDTH), BF16),
        ((SECTIONS, ROWS, WIDTH), BF16),
        ((SECTIONS, ROWS, WIDTH), BF16),
        ((SECTIONS, ROWS, WIDTH), BF16),
        ((SECTIONS, 2 * HALF, WIDTH), BF16),
        ((SECTIONS, HALF, WIDTH), BF16),
        ((SECTIONS, COL, WIDTH), BF16),
        ((SECTIONS, COL, WIDTH), BF16),
        ((SECTIONS, COL, WIDTH), BF16),
        ((SECTIONS, 2 * HALF, WIDTH), F32),
        ((SECTIONS, HALF, WIDTH), F32),
        ((SECTIONS, HALF, WIDTH), BF16),
        ((SECTIONS, HALF, WIDTH), BF16),
        ((SECTIONS, 2 * HALF, WIDTH), F32),
        ((ROWS, WIDTH), F32),
        ((2,) + part, BF16),
        ((2, 2) + part, BF16),
        ((2,) + part, BF16),
        ((2, 2) + part, BF16),
        ((2, QUART, BLOCK), BF16),
        ((2, 2, QUART, BLOCK), BF16),
        ((2, QUART, BLOCK), BF16),
        ((2, 2, QUART, BLOCK), BF16),
        ((2, 3, CHUNK, COL), BF16),
    ]
    proj, hgrad, fgrad = pl.pallas_call(
        kernel,
        out_shape=(
            jax.ShapeDtypeStruct((ROWS, COL), BF16),
            jax.ShapeDtypeStruct((ROWS, WIDTH), BF16),
            jax.ShapeDtypeStruct((SECTIONS, 2 * HALF, WIDTH), F32),
        ),
        in_specs=[vmem, pl.BlockSpec(memory_space=pl.ANY), vmem, vmem],
        out_specs=(vmem, vmem, vmem),
        scratch_shapes=[pltpu.VMEM(*one) for one in scratch]
        + [
            pltpu.SemaphoreType.DMA((SIDE * SIDE,)),
            pltpu.SemaphoreType.DMA((COPIES,)),
            pltpu.SemaphoreType.DMA((COPIES,)),
        ],
        compiler_params=pltpu.CompilerParams(
            collective_id=0, has_side_effects=True, vmem_limit_bytes=56 * 1024 * 1024
        ),
        name="butterfly",
    )(hidden, weight, factors, cotangent)
    grad = fgrad.reshape(SECTIONS, 2 * HALF, 7, 2 * HALF).transpose(0, 2, 1, 3)
    tokens = ROWS * lax.axis_size("dp")
    return proj, hgrad, grad / jnp.float32(tokens)


def solution(mesh):
    return jax.shard_map(
        body,
        mesh=mesh,
        in_specs=(
            P("dp", "tensor"),
            P("tensor", None),
            P(None, "tensor", None, None),
            P("dp", "tensor"),
        ),
        out_specs=(P("dp", "tensor"), P("dp", "tensor"), P(None, "tensor", None, None)),
        check_vma=False,
    )
```

time: 865 us -> 138 us (0.16)
  the two profiles are of different devices: /device:TPU:0 before, /device:TPU:1 now
where the time goes in v1:
time: 138 us; the launch traced here: 136 us
  Pallas kernels  129 us (93%)
  local copies, waits for them, and re-layouts  5.87 us (4%)
    pallas_call x1, Pallas kernels, body(): pl.pallas_call(kernel, out_shape=(jax.ShapeDtypeStruct((ROWS, COL), BF16)...  129 us
    unnamed x6, local copies, waits for them, and re-layouts  5.51 us

profile of v1, /device:TPU:1, one launch (start us, length us, event | category | flops | bytes accessed | tf_op | source)
XLA Modules:
  0.0 136.5 jit_solution(9432087951390229310)
XLA Ops:
  0.6 1.8 %copy.10.hid = bf16[256,448]{1,0:T(8,128)(2,1)} copy(bf16[256,448]{0,1:T(8,128)(2,1)} %param.4) | data formatting | bytes 458752 | tf_op args[0]
  2.4 128.8 %butterfly.1 = (bf16[256,128]{1,0:T(8,128)(2,1)}, bf16[256,448]{1,0:T(8,128)(2,1)}, f32[6,64,448]{2,1,0:T(8,128)}) custom-call(bf16[256,448]{1,0:T(8,128)(2,1)} %copy.10.hid, bf16[448,8192]{1,0:T(8,128)(2,1)} %w_hbm.1, bf16[6,7,64,64]{3,2,1,0:T(8,128)(2,1)} %fac.1, bf16[256,128]{1,0:T(8,128)(2,1)} %cot.1), custom_call_target="tpu_custom_call" | custom-call | tf_op jit(solution)/shard_map/butterfly/pallas_call | solution.py:390
  131.2 1.8 %copy.11 = bf16[256,448]{0,1:T(8,128)(2,1)} copy(bf16[256,448]{1,0:T(8,128)(2,1)} %get-tuple-element.13) | data formatting | bytes 458752
  133.0 1.2 broadcast_multiply_fusion
  134.2 0.4 div.12
  134.5 0.0 copy-start
  134.5 1.3 copy.12
  135.9 0.0 copy-done
  135.9 0.6 copy.14
Async XLA Ops:
  134.5 1.3 copy-start

commit v2 on v1

v2 whole, which is shorter than its diff:
```python
import jax
import jax.numpy as jnp
from jax import lax
from jax.experimental import pallas as pl
from jax.experimental.pallas import tpu as pltpu
from jax.sharding import PartitionSpec as P

MESH = pl.DeviceIdType.MESH
BF16 = jnp.bfloat16
F32 = jnp.float32

ROWS = 256
WIDTH = 448
LANES = 7
HALF = 32
SECTIONS = 6
SIDE = 4
COL = 128
BLOCK = SIDE * COL
CHUNK = 128
QUART = 64
TILES = ((0, 128), (128, 128), (256, 128), (384, 64))
PARTS = ((0, 1), (2, 3))

SCHEDULE = (
    ("G", "F0", "F1", "S", "F0", "F1", "G", "F0", "F1", "G", "F0", "F1", "G", "F0", "F1"),
    ("F0", "F1", "G", "G", "B0", "B1", "F0", "F1", "R"),
    ("D5", "B0", "B1", "D4", "D5", "R", "B0", "B1", "D3", "D4", "D5", "R"),
    ("B0", "B1", "D2", "D3", "D4", "R", "B0", "B1", "D1", "D2", "D3", "R"),
    ("B0", "B1", "D0", "D1", "D2", "D0", "D1", "B0", "B1", "D0"),
)


def dot(a, b, contract=((1,), (0,))):
    return lax.dot_general(a, b, (contract, ((), ())), preferred_element_type=F32)


NT = ((1,), (1,))


def kernel(
    hid, w_hbm, fac_hbm, cot_hbm, proj_out, hgrad_out, fgrad_out,
    wv, cotv, facv, cotg, par, xs, xp, gs, gp, fac_t, fac_p, ma, mat, mbt, mp,
    fg, fg_core, fg_half, fg_far, fg_all, acc, ra1, ra2, rb1, rb2, sa, sb, zr,
    proj, hgrad, fgrad, in_sem, out_sem, send, recv,
):
    dp = lax.axis_index("dp")
    t = lax.axis_index("tensor")
    y = lax.div(t, SIDE * SIDE)
    x = lax.rem(lax.div(t, SIDE), SIDE)
    z = lax.rem(t, SIDE)
    core = lax.rem(dp, 2)

    def ring(v, k):
        return lax.rem(v + k, SIDE)

    def at(yy, xx, zz):
        return (dp, (yy * SIDE + xx) * SIDE + zz)

    def y_dev(k):
        return at(ring(y, k), x, z)

    def x_dev(k):
        return at(y, ring(x, k), z)

    def z_dev(k):
        return at(y, x, ring(z, k))

    far = lax.rem(dp + 2, 4)
    core_dev = (dp + 1 - 2 * core, t)
    far_dev = (far, t)
    cross_dev = (far + 1 - 2 * core, t)

    def bit_of(s):
        return lax.rem(lax.div(t, 1 << s), 2)

    def partner(s):
        return (dp, t + (1 << s) * (1 - 2 * bit_of(s)))

    def own_rows(s):
        return pl.ds(pl.multiple_of(HALF * bit_of(s), HALF), HALF)

    def other_rows(s):
        return pl.ds(pl.multiple_of(HALF - HALF * bit_of(s), HALF), HALF)

    started = []

    def copy(src, dst, dev):
        k = len(started)
        c = pltpu.make_async_remote_copy(
            src_ref=src, dst_ref=dst, send_sem=send.at[k], recv_sem=recv.at[k],
            device_id=dev, device_id_type=MESH,
        )
        c.start()
        started.append(c)
        return c

    def fetch(src, dst, k):
        c = pltpu.make_async_copy(src, dst, in_sem.at[k])
        c.start()
        return c

    cot_copy = fetch(cot_hbm, cotv, 0)
    hid_copy = fetch(hid, xs.at[0], 1)
    fac_copy = fetch(fac_hbm, facv, 2)
    w_copies = [
        fetch(w_hbm.at[:, pl.ds(b * BLOCK, BLOCK)], wv.at[b], 3 + b) for b in range(SIDE * SIDE)
    ]
    stored = []

    def put(src, dst):
        c = pltpu.make_async_copy(src, dst, out_sem.at[len(stored)])
        c.start()
        stored.append(c)

    peers = [f(k) for f in (z_dev, x_dev, y_dev) for k in (1, 2, 3)]
    peers += [core_dev, far_dev, cross_dev]
    barrier = pltpu.get_barrier_semaphore()
    for dev in peers:
        pl.semaphore_signal(barrier, inc=1, device_id=dev, device_id_type=MESH)
    pl.semaphore_wait(barrier, len(peers))

    half_a, half_b = pl.ds(0, CHUNK), pl.ds(CHUNK, CHUNK)
    rows_a = (pl.ds(0, QUART), pl.ds(QUART, QUART))
    rows_b = (pl.ds(CHUNK, QUART), pl.ds(CHUNK + QUART, QUART))

    def gather_phase(view, i, dev):
        r1 = copy(view(i, 0), view(i, 0), dev(1))
        l2 = copy(view(i, 1), view(i, 1), dev(3))
        r2 = copy(view(i, 1), view(i, 1), dev(1))
        l1 = copy(view(i, 0), view(i, 0), dev(3))
        yield
        left, right = ring(i, 3), ring(i, 1)
        r1.wait_recv()
        far1 = copy(view(left, 0), view(left, 0), dev(1))
        l2.wait_recv()
        far2 = copy(view(right, 1), view(right, 1), dev(3))
        yield
        r2.wait_recv()
        l1.wait_recv()
        yield
        far1.wait_recv()
        far2.wait_recv()
        yield

    def grad_dots(n, place):
        def step(k, carry):
            yy, xx = place(k)
            acc[...] += dot(wv[yy * SIDE + xx], cotg[yy, xx], NT)
            return carry

        lax.fori_loop(0, n, step, 0)

    def columns(zz):
        return pl.ds(pl.multiple_of(zz * COL, COL), COL)

    def gather():
        cot_copy.wait()
        copies = [copy(cotv, cotg.at[y, x, :, columns(z)], z_dev(k)) for k in (1, 2, 3)]
        cotg[y, x, :, columns(z)] = cotv[...]
        acc[...] = jnp.zeros_like(acc)
        yield
        for c in copies:
            c.wait_recv()
        here_a, here_b = cotg.at[y, x, half_a, :], cotg.at[y, x, half_b, :]
        copies = []
        for k in (1, 3, 2):
            copies.append(copy(here_a, here_a, x_dev(k)))
            copies.append(copy(here_b, here_b, y_dev(k)))
        yield
        for c in copies:
            c.wait_recv()
        pa = gather_phase(lambda i, h: cotg.at[i, :, rows_a[h], :], y, y_dev)
        pb = gather_phase(lambda i, h: cotg.at[:, i, rows_b[h], :], x, x_dev)
        next(pa), next(pb)
        yield
        next(pa), next(pb)
        yield
        next(pa), next(pb)
        for c in w_copies:
            c.wait()
        grad_dots(9, lambda k: (ring(y, 3 + lax.div(k, 3)), ring(x, 3 + lax.rem(k, 3))))
        yield
        next(pa), next(pb)
        grad_dots(
            7,
            lambda k: (
                ring(y, jnp.where(k < 4, 2, k - 1)),
                ring(x, jnp.where(k < 4, k, 2)),
            ),
        )
        gs[SECTIONS - 1] = acc[...].astype(BF16)
        yield

    diag = (
        lax.broadcasted_iota(jnp.int32, (COL, WIDTH), 0) // HALF
        == lax.rem(lax.broadcasted_iota(jnp.int32, (COL, WIDTH), 1), COL) // HALF
    )

    def spread(part):
        return jnp.where(diag, jnp.concatenate([part] * 4, axis=0), jnp.zeros((), BF16))

    def turned(ref, full):
        for lo, w in TILES:
            ref[lo : lo + w, 0:w] = full[0:w, lo : lo + w].T

    fac_copies = [None] * SECTIONS

    def setup():
        fac_copy.wait()
        for s in range(SECTIONS):
            fac_t[s] = jnp.concatenate([facv[s, j] for j in range(LANES)], axis=1)
        for s in reversed(range(SECTIONS)):
            fac_copies[s] = copy(fac_t.at[s, other_rows(s), :], fac_p.at[s], partner(s))
        for s in range(SECTIONS):
            own = spread(fac_t[s, own_rows(s), :])
            ma[s] = own
            turned(mat.at[s], own)
            turned(mbt.at[s], spread(fac_t[s, other_rows(s), :]))
        yield

    def span(part):
        lo = TILES[part[0]][0]
        return pl.ds(lo, TILES[part[-1]][0] + TILES[part[-1]][1] - lo)

    def forward(part):
        if part is PARTS[0]:
            hid_copy.wait()
        for s in range(SECTIONS):
            rows = span(part)
            c = copy(xs.at[s, rows, :], xp.at[s, rows, :], partner(s))
            yield
            c.wait_recv()
            for i in part:
                lo, w = TILES[i]
                own = xs[s, lo : lo + w, :]
                mix = dot(mat[s, lo : lo + w, 0:w], own)
                mix += dot(mbt[s, lo : lo + w, 0:w], xp[s, lo : lo + w, :])
                xs[s + 1, lo : lo + w, :] = (own.astype(F32) + mix).astype(BF16)
        yield

    def proj_dots(n, place):
        def step(k, carry):
            yy, xx = place(k)
            par[yy, xx] = dot(proj_in[0], wv[yy * SIDE + xx]).astype(BF16)
            return carry

        lax.fori_loop(0, n, step, 0)

    proj_in = [None]

    def add_to(ref, *others):
        total = ref[...].astype(F32)
        for o in others:
            total += o[...].astype(F32)
        ref[...] = total.astype(BF16)

    def scatter_phase(view, i, buf1, buf2, dev):
        p1, p2, m1 = ring(i, 1), ring(i, 2), ring(i, 3)
        a = copy(view(p2, 0), buf1.at[0], dev(1))
        b = copy(view(p2, 1), buf1.at[1], dev(3))
        yield
        c = copy(view(p1, 1), buf2.at[0, 1], dev(1))
        d = copy(view(m1, 0), buf2.at[1, 0], dev(3))
        yield
        a.wait_recv()
        add_to(view(p1, 0), buf1.at[0])
        e = copy(view(p1, 0), buf2.at[0, 0], dev(1))
        b.wait_recv()
        add_to(view(m1, 1), buf1.at[1])
        f = copy(view(m1, 1), buf2.at[1, 1], dev(3))
        yield
        c.wait_recv()
        f.wait_recv()
        add_to(view(i, 1), buf2.at[0, 1], buf2.at[1, 1])
        d.wait_recv()
        e.wait_recv()
        add_to(view(i, 0), buf2.at[0, 0], buf2.at[1, 0])
        yield

    def scatter():
        pa = scatter_phase(lambda i, h: par.at[i, :, rows_a[h], :], y, ra1, ra2, y_dev)
        pb = scatter_phase(lambda i, h: par.at[:, i, rows_b[h], :], x, rb1, rb2, x_dev)
        proj_in[0] = xs[SECTIONS].T
        proj_dots(4, lambda k: (ring(y, 2), ring(x, k)))
        next(pa)
        proj_dots(3, lambda k: (ring(y, 3 + k), ring(x, 2)))
        next(pb)
        proj_dots(6, lambda k: (ring(y, 1 + 2 * lax.div(k, 3)), ring(x, 3 + lax.rem(k, 3))))
        next(pa)
        proj_dots(3, lambda k: (y, ring(x, 3 + k)))
        next(pb)
        yield
        next(pa), next(pb)
        yield
        next(pa), next(pb)
        copies = []
        for k in (2, 1, 3):
            copies.append(copy(par.at[y, ring(x, k), half_a, :], sa.at[k - 1], x_dev(k)))
            copies.append(copy(par.at[ring(y, k), x, half_b, :], sb.at[k - 1], y_dev(k)))
        yield
        for c in copies:
            c.wait_recv()
        add_to(par.at[y, x, half_a, :], sa.at[0], sa.at[1], sa.at[2])
        add_to(par.at[y, x, half_b, :], sb.at[0], sb.at[1], sb.at[2])
        copies = [
            copy(par.at[y, x, :, columns(ring(z, k))], zr.at[k - 1], z_dev(k)) for k in (1, 2, 3)
        ]
        yield
        total = par[y, x, :, columns(z)].astype(F32)
        for k in (1, 2, 3):
            copies[k - 1].wait_recv()
            total += zr[k - 1].astype(F32)
        proj[...] = total.astype(BF16)
        put(proj, proj_out)
        yield

    def backward(part):
        for s in reversed(range(SECTIONS)):
            rows = span(part)
            c = copy(gs.at[s, rows, :], gp.at[s, rows, :], partner(s))
            if part is PARTS[0]:
                fac_copies[s].wait_recv()
                mp[s] = spread(fac_p[s])
            yield
            c.wait_recv()
            for i in part:
                lo, w = TILES[i]
                own = gs[s, lo : lo + w, :]
                back = dot(ma[s, 0:w, lo : lo + w], own)
                back += dot(mp[s, 0:w, lo : lo + w], gp[s, lo : lo + w, :])
                new = (own.astype(F32) + back).astype(BF16)
                if s == 0:
                    hgrad[lo : lo + w, :] = new
                else:
                    gs[s - 1, lo : lo + w, :] = new
        put(hgrad.at[rows, :], hgrad_out.at[rows, :])
        yield

    keep = pl.ds(pl.multiple_of(HALF * core, HALF), HALF)
    give = pl.ds(pl.multiple_of(HALF - HALF * core, HALF), HALF)

    def factor(s):
        for act, rows in ((xs.at[s], own_rows(s)), (xp.at[s], other_rows(s))):
            for lo, w in TILES:
                full = dot(act[lo : lo + w, :], gs[s, lo : lo + w, :], NT)
                full = jnp.where(diag[:w, :w], full, 0.0)
                total = full[0:HALF]
                for g in range(1, w // HALF):
                    total += full[g * HALF : (g + 1) * HALF]
                fg[s, rows, lo : lo + w] = total
        if s == 0:
            a = copy(fg.at[s], fg_all.at[s], core_dev)
            yield
            a.wait_recv()
            chip = (fg[s] + fg_all[s]).astype(BF16)
            fg_half[...] = chip
            b = copy(fg_half.at[keep, :], fg_far.at[s, keep, :], far_dev)
            c = copy(fg_half.at[keep, :], fg_far.at[s, keep, :], cross_dev)
            yield
            b.wait_recv()
            c.wait_recv()
            total = chip.astype(F32) + fg_far[s].astype(F32)
        else:
            a = copy(fg.at[s, give, :], fg_core.at[s], core_dev)
            yield
            a.wait_recv()
            chip = (fg[s, keep, :] + fg_core[s]).astype(BF16)
            fg_far[s, give, :] = chip
            b = copy(fg_far.at[s, give, :], fg_far.at[s, keep, :], far_dev)
            yield
            b.wait_recv()
            fg_all[s, keep, :] = chip.astype(F32) + fg_far[s, keep, :].astype(F32)
            c = copy(fg_all.at[s, keep, :], fg_all.at[s, keep, :], core_dev)
            yield
            c.wait_recv()
            total = fg_all[s]
        total = total * (1.0 / (4 * ROWS))
        for j in range(LANES):
            fgrad[s, j] = total[:, 2 * HALF * j : 2 * HALF * (j + 1)]
        put(fgrad.at[s], fgrad_out.at[s])
        yield

    chains = {"G": gather(), "S": setup(), "R": scatter()}
    for n, part in enumerate(PARTS):
        chains[f"F{n}"] = forward(part)
        chains[f"B{n}"] = backward(part)
    for s in range(SECTIONS):
        chains[f"D{s}"] = factor(s)
    for name in sum(SCHEDULE, ()):
        next(chains[name], None)
    for chain in chains.values():
        for _ in chain:
            pass
    assert len(started) == COPIES
    for c in started:
        c.wait_send()
    for c in stored:
        c.wait()


COPIES = 3 + 6 + 12 + 6 + 12 * len(PARTS) + 12 + 6 + 3 + 18
STORES = 1 + len(PARTS) + SECTIONS


def body(hidden, weight, factors, cotangent):
    anywhere = pl.BlockSpec(memory_space=pl.ANY)
    part = (SIDE, QUART, BLOCK)
    acts = (SECTIONS, WIDTH, ROWS)
    scratch = [
        ((SIDE * SIDE, WIDTH, BLOCK), BF16),
        ((ROWS, COL), BF16),
        ((SECTIONS, LANES, 2 * HALF, 2 * HALF), BF16),
        ((SIDE, SIDE, ROWS, BLOCK), BF16),
        ((SIDE, SIDE, ROWS, BLOCK), BF16),
        ((SECTIONS + 1, WIDTH, ROWS), BF16),
        (acts, BF16),
        (acts, BF16),
        (acts, BF16),
        ((SECTIONS, 2 * HALF, WIDTH), BF16),
        ((SECTIONS, HALF, WIDTH), BF16),
        ((SECTIONS, COL, WIDTH), BF16),
        ((SECTIONS, WIDTH, COL), BF16),
        ((SECTIONS, WIDTH, COL), BF16),
        ((SECTIONS, COL, WIDTH), BF16),
        ((SECTIONS, 2 * HALF, WIDTH), F32),
        ((SECTIONS, HALF, WIDTH), F32),
        ((2 * HALF, WIDTH), BF16),
        ((SECTIONS, 2 * HALF, WIDTH), BF16),
        ((SECTIONS, 2 * HALF, WIDTH), F32),
        ((WIDTH, ROWS), F32),
        ((2,) + part, BF16),
        ((2, 2) + part, BF16),
        ((2,) + part, BF16),
        ((2, 2) + part, BF16),
        ((3, CHUNK, BLOCK), BF16),
        ((3, CHUNK, BLOCK), BF16),
        ((3, ROWS, COL), BF16),
        ((ROWS, COL), BF16),
        ((WIDTH, ROWS), BF16),
        ((SECTIONS, LANES, 2 * HALF, 2 * HALF), F32),
    ]
    proj, hgrad, fgrad = pl.pallas_call(
        kernel,
        out_shape=(
            jax.ShapeDtypeStruct((ROWS, COL), BF16),
            jax.ShapeDtypeStruct((WIDTH, ROWS), BF16),
            jax.ShapeDtypeStruct((SECTIONS, LANES, 2 * HALF, 2 * HALF), F32),
        ),
        in_specs=[anywhere] * 4,
        out_specs=(anywhere,) * 3,
        scratch_shapes=[pltpu.VMEM(*one) for one in scratch]
        + [
            pltpu.SemaphoreType.DMA((3 + SIDE * SIDE,)),
            pltpu.SemaphoreType.DMA((STORES,)),
            pltpu.SemaphoreType.DMA((COPIES,)),
            pltpu.SemaphoreType.DMA((COPIES,)),
        ],
        compiler_params=pltpu.CompilerParams(
            collective_id=0, has_side_effects=True, vmem_limit_bytes=56 * 1024 * 1024
        ),
        name="butterfly",
    )(hidden.T, weight, factors, cotangent)
    return proj, hgrad.T, fgrad


def solution(mesh):
    return jax.shard_map(
        body,
        mesh=mesh,
        in_specs=(
            P("dp", "tensor"),
            P("tensor", None),
            P(None, "tensor", None, None),
            P("dp", "tensor"),
        ),
        out_specs=(P("dp", "tensor"), P("dp", "tensor"), P(None, "tensor", None, None)),
        check_vma=False,
    )
```

time: 138 us -> 128 us (0.928)
  Pallas kernels: 129 us -> 121 us
    pallas_call x1, Pallas kernels: 129 us -> 121 us  [body(): pl.pallas_call(kernel, out_shape=(jax.ShapeDtypeStruct((ROWS, COL), BF16)...]
    unnamed x6 -> x3, local copies, waits for them, and re-layouts: 5.51 us -> 5.68 us
where the time goes in v2:
time: 128 us
  Pallas kernels  121 us (95%)
  local copies, waits for them, and re-layouts  5.68 us (4%)
    pallas_call x1, Pallas kernels, body(): pl.pallas_call(kernel, out_shape=(jax.ShapeDtypeStruct((ROWS, COL), BF16)...  121 us
    unnamed x3, local copies, waits for them, and re-layouts  5.68 us

profile of v2, /device:TPU:1, one launch (start us, length us, event | category | flops | bytes accessed | tf_op | source)
XLA Modules:
  0.0 127.5 jit_solution(8487579310392090736)
XLA Ops:
  0.6 121.2 %butterfly.1 = (bf16[256,128]{1,0:T(8,128)(2,1)}, bf16[448,256]{1,0:T(8,128)(2,1)}, f32[6,7,64,64]{3,2,1,0:T(8,128)}) custom-call(bf16[448,256]{1,0:T(8,128)(2,1)} %bitcast.3, bf16[448,8192]{1,0:T(8,128)(2,1)} %w_hbm.1, bf16[6,7,64,64]{3,2,1,0:T(8,128)(2,1)} %fac_hbm.1, bf16[256,128]{1,0:T(8,128)(2,1)} %cot_hbm.1), custom_call_target="tpu_custom_call" | custom-call | tf_op jit(solution)/shard_map/butterfly/pallas_call | solution.py:443
  121.8 1.5 %copy.10 = bf16[256,128]{1,0:T(8,128)(2,1)} copy(bf16[256,128]{1,0:T(8,128)(2,1)} %get-tuple-element.12) | data formatting | bytes 131072
  123.3 1.6 %copy.11 = bf16[256,448]{0,1:T(8,128)(2,1)} copy(bf16[256,448]{0,1:T(8,128)(2,1)} %bitcast.2) | data formatting | bytes 458752
  124.9 2.6 %copy.12 = f32[6,7,64,64]{3,2,1,0:T(8,128)} copy(f32[6,7,64,64]{3,2,1,0:T(8,128)} %get-tuple-element.14) | data formatting | bytes 1376256

commit v3 on v2

--- a/solution.py
+++ b/solution.py
@@ -18,16 +18,23 @@
 COL = 128
 BLOCK = SIDE * COL
 CHUNK = 128
-QUART = 64
 TILES = ((0, 128), (128, 128), (256, 128), (384, 64))
-PARTS = ((0, 1), (2, 3))
+PARTS = ((0,), (1,), (2, 3))
+
+GROUPS = 2
 
 SCHEDULE = (
-    ("G", "F0", "F1", "S", "F0", "F1", "G", "F0", "F1", "G", "F0", "F1", "G", "F0", "F1"),
-    ("F0", "F1", "G", "G", "B0", "B1", "F0", "F1", "R"),
-    ("D5", "B0", "B1", "D4", "D5", "R", "B0", "B1", "D3", "D4", "D5", "R"),
-    ("B0", "B1", "D2", "D3", "D4", "R", "B0", "B1", "D1", "D2", "D3", "R"),
-    ("B0", "B1", "D0", "D1", "D2", "D0", "D1", "B0", "B1", "D0"),
+    ("G", "F2", "S", "F1", "F0", "G", "GB0", "GA0", "GB1", "GA1"),
+    ("F0", "GA0", "GB1", "F2", "F1", "GB0", "GA1", "GA1", "F0", "GB0"),
+    ("GB1", "GA0", "GD", "GA0", "GB1", "GB0", "GA1", "GD", "B0", "F2"),
+    ("B1", "F0", "B2", "F2", "B0", "F1", "F0", "B1", "B2", "B0"),
+    ("F2", "F1", "B0", "F0", "B2", "F1", "B1", "B0", "D3", "F2"),
+    ("B2", "F1", "F2", "B1", "D3", "F0", "D4", "F1", "R", "R"),
+    ("B1", "B2", "D5", "R", "R", "RA0", "B0", "D2", "B1", "D3"),
+    ("D5", "RB1", "RB0", "D1", "B0", "B2", "D0", "D1", "RA1", "D5"),
+    ("D3", "D2", "D0", "RB1", "D4", "RA0", "D2", "D5", "RB0", "RA1"),
+    ("D1", "RB1", "RA0", "RB0", "RA1", "D0", "D4", "D2", "RB1", "RB0"),
+    ("RA0", "B1", "B2", "D1", "D4", "RA1"),
 )
 
 
@@ -41,7 +48,7 @@
 def kernel(
     hid, w_hbm, fac_hbm, cot_hbm, proj_out, hgrad_out, fgrad_out,
     wv, cotv, facv, cotg, par, xs, xp, gs, gp, fac_t, fac_p, ma, mat, mbt, mp,
-    fg, fg_core, fg_half, fg_far, fg_all, acc, ra1, ra2, rb1, rb2, sa, sb, zr,
+    fg, fg_core, fg_half, fg_far, fg_all, acc, buf1, buf2, buf3, zr,
     proj, hgrad, fgrad, in_sem, out_sem, send, recv,
 ):
     dp = lax.axis_index("dp")
@@ -120,9 +127,14 @@
         pl.semaphore_signal(barrier, inc=1, device_id=dev, device_id_type=MESH)
     pl.semaphore_wait(barrier, len(peers))
 
-    half_a, half_b = pl.ds(0, CHUNK), pl.ds(CHUNK, CHUNK)
-    rows_a = (pl.ds(0, QUART), pl.ds(QUART, QUART))
-    rows_b = (pl.ds(CHUNK, QUART), pl.ds(CHUNK + QUART, QUART))
+    size = CHUNK // GROUPS
+    piece = size // 2
+
+    def group(h, g):
+        return pl.ds(CHUNK * h + size * g, size)
+
+    def piece_of(h, g, p):
+        return pl.ds(CHUNK * h + size * g + piece * p, piece)
 
     def gather_phase(view, i, dev):
         r1 = copy(view(i, 0), view(i, 0), dev(1))
@@ -154,6 +166,8 @@
     def columns(zz):
         return pl.ds(pl.multiple_of(zz * COL, COL), COL)
 
+    second = {}
+
     def gather():
         cot_copy.wait()
         copies = [copy(cotv, cotg.at[y, x, :, columns(z)], z_dev(k)) for k in (1, 2, 3)]
@@ -162,26 +176,25 @@
         yield
         for c in copies:
             c.wait_recv()
-        here_a, here_b = cotg.at[y, x, half_a, :], cotg.at[y, x, half_b, :]
-        copies = []
-        for k in (1, 3, 2):
-            copies.append(copy(here_a, here_a, x_dev(k)))
-            copies.append(copy(here_b, here_b, y_dev(k)))
-        yield
-        for c in copies:
-            c.wait_recv()
-        pa = gather_phase(lambda i, h: cotg.at[i, :, rows_a[h], :], y, y_dev)
-        pb = gather_phase(lambda i, h: cotg.at[:, i, rows_b[h], :], x, x_dev)
-        next(pa), next(pb)
-        yield
-        next(pa), next(pb)
-        yield
-        next(pa), next(pb)
+        for g in range(GROUPS):
+            here = [cotg.at[y, x, group(h, g), :] for h in (0, 1)]
+            second[0, g] = [copy(here[0], here[0], x_dev(k)) for k in (1, 3, 2)]
+            second[1, g] = [copy(here[1], here[1], y_dev(k)) for k in (1, 3, 2)]
+        yield
+
+    def gather_group(h, g):
+        for c in second[h, g]:
+            c.wait_recv()
+        if h == 0:
+            yield from gather_phase(lambda i, p: cotg.at[i, :, piece_of(h, g, p), :], y, y_dev)
+        else:
+            yield from gather_phase(lambda i, p: cotg.at[:, i, piece_of(h, g, p), :], x, x_dev)
+
+    def gather_dots():
         for c in w_copies:
             c.wait()
         grad_dots(9, lambda k: (ring(y, 3 + lax.div(k, 3)), ring(x, 3 + lax.rem(k, 3))))
         yield
-        next(pa), next(pb)
         grad_dots(
             7,
             lambda k: (
@@ -223,9 +236,12 @@
         lo = TILES[part[0]][0]
         return pl.ds(lo, TILES[part[-1]][0] + TILES[part[-1]][1] - lo)
 
+    loaded = []
+
     def forward(part):
-        if part is PARTS[0]:
+        if not loaded:
             hid_copy.wait()
+            loaded.append(True)
         for s in range(SECTIONS):
             rows = span(part)
             c = copy(xs.at[s, rows, :], xp.at[s, rows, :], partner(s))
@@ -255,73 +271,90 @@
             total += o[...].astype(F32)
         ref[...] = total.astype(BF16)
 
-    def scatter_phase(view, i, buf1, buf2, dev):
-        p1, p2, m1 = ring(i, 1), ring(i, 2), ring(i, 3)
-        a = copy(view(p2, 0), buf1.at[0], dev(1))
-        b = copy(view(p2, 1), buf1.at[1], dev(3))
-        yield
-        c = copy(view(p1, 1), buf2.at[0, 1], dev(1))
-        d = copy(view(m1, 0), buf2.at[1, 0], dev(3))
-        yield
+    def sum_view(h, g):
+        if h == 0:
+            return lambda i, p: par.at[i, :, piece_of(h, g, p), :]
+        return lambda i, p: par.at[:, i, piece_of(h, g, p), :]
+
+    first = {(h, g): [] for h in (0, 1) for g in range(GROUPS)}
+
+    def send_far(h):
+        i, dev = ((y, y_dev), (x, x_dev))[h]
+        for g in range(GROUPS):
+            view = sum_view(h, g)
+            first[h, g].append(copy(view(ring(i, 2), 0), buf1.at[h, g, 0], dev(1)))
+            first[h, g].append(copy(view(ring(i, 2), 1), buf1.at[h, g, 1], dev(3)))
+
+    def send_near(h):
+        i, dev = ((y, y_dev), (x, x_dev))[h]
+        for g in range(GROUPS):
+            view = sum_view(h, g)
+            first[h, g].append(copy(view(ring(i, 1), 1), buf2.at[h, g, 0, 1], dev(1)))
+            first[h, g].append(copy(view(ring(i, 3), 0), buf2.at[h, g, 1, 0], dev(3)))
+
+    def scatter():
+        proj_in[0] = xs[SECTIONS].T
+        proj_dots(4, lambda k: (ring(y, 2), ring(x, k)))
+        send_far(0)
+        yield
+        proj_dots(3, lambda k: (ring(y, 3 + k), ring(x, 2)))
+        send_far(1)
+        yield
+        proj_dots(6, lambda k: (ring(y, 1 + 2 * lax.div(k, 3)), ring(x, 3 + lax.rem(k, 3))))
+        send_near(0)
+        yield
+        proj_dots(3, lambda k: (y, ring(x, 3 + k)))
+        send_near(1)
+        yield
+
+    def scatter_group(h, g):
+        view, rows = sum_view(h, g), group(h, g)
+        i, dev, dev2 = ((y, y_dev, x_dev), (x, x_dev, y_dev))[h]
+        a, b, c, d = first[h, g]
         a.wait_recv()
-        add_to(view(p1, 0), buf1.at[0])
-        e = copy(view(p1, 0), buf2.at[0, 0], dev(1))
+        add_to(view(ring(i, 1), 0), buf1.at[h, g, 0])
+        e = copy(view(ring(i, 1), 0), buf2.at[h, g, 0, 0], dev(1))
         b.wait_recv()
-        add_to(view(m1, 1), buf1.at[1])
-        f = copy(view(m1, 1), buf2.at[1, 1], dev(3))
+        add_to(view(ring(i, 3), 1), buf1.at[h, g, 1])
+        f = copy(view(ring(i, 3), 1), buf2.at[h, g, 1, 1], dev(3))
         yield
         c.wait_recv()
         f.wait_recv()
-        add_to(view(i, 1), buf2.at[0, 1], buf2.at[1, 1])
+        add_to(view(i, 1), buf2.at[h, g, 0, 1], buf2.at[h, g, 1, 1])
         d.wait_recv()
         e.wait_recv()
-        add_to(view(i, 0), buf2.at[0, 0], buf2.at[1, 0])
-        yield
-
-    def scatter():
-        pa = scatter_phase(lambda i, h: par.at[i, :, rows_a[h], :], y, ra1, ra2, y_dev)
-        pb = scatter_phase(lambda i, h: par.at[:, i, rows_b[h], :], x, rb1, rb2, x_dev)
-        proj_in[0] = xs[SECTIONS].T
-        proj_dots(4, lambda k: (ring(y, 2), ring(x, k)))
-        next(pa)
-        proj_dots(3, lambda k: (ring(y, 3 + k), ring(x, 2)))
-        next(pb)
-        proj_dots(6, lambda k: (ring(y, 1 + 2 * lax.div(k, 3)), ring(x, 3 + lax.rem(k, 3))))
-        next(pa)
-        proj_dots(3, lambda k: (y, ring(x, 3 + k)))
-        next(pb)
-        yield
-        next(pa), next(pb)
-        yield
-        next(pa), next(pb)
+        add_to(view(i, 0), buf2.at[h, g, 0, 0], buf2.at[h, g, 1, 0])
         copies = []
         for k in (2, 1, 3):
-            copies.append(copy(par.at[y, ring(x, k), half_a, :], sa.at[k - 1], x_dev(k)))
-            copies.append(copy(par.at[ring(y, k), x, half_b, :], sb.at[k - 1], y_dev(k)))
+            src = par.at[y, ring(x, k), rows, :] if h == 0 else par.at[ring(y, k), x, rows, :]
+            copies.append(copy(src, buf3.at[h, g, k - 1], dev2(k)))
         yield
         for c in copies:
             c.wait_recv()
-        add_to(par.at[y, x, half_a, :], sa.at[0], sa.at[1], sa.at[2])
-        add_to(par.at[y, x, half_b, :], sb.at[0], sb.at[1], sb.at[2])
+        add_to(par.at[y, x, rows, :], *[buf3.at[h, g, k] for k in range(3)])
         copies = [
-            copy(par.at[y, x, :, columns(ring(z, k))], zr.at[k - 1], z_dev(k)) for k in (1, 2, 3)
+            copy(par.at[y, x, rows, columns(ring(z, k))], zr.at[h, g, k - 1], z_dev(k))
+            for k in (1, 2, 3)
         ]
         yield
-        total = par[y, x, :, columns(z)].astype(F32)
+        total = par[y, x, rows, columns(z)].astype(F32)
         for k in (1, 2, 3):
             copies[k - 1].wait_recv()
-            total += zr[k - 1].astype(F32)
-        proj[...] = total.astype(BF16)
-        put(proj, proj_out)
-        yield
+            total += zr[h, g, k - 1].astype(F32)
+        proj[rows, :] = total.astype(BF16)
+        put(proj.at[rows, :], proj_out.at[rows, :])
+        yield
+
+    joined = []
 
     def backward(part):
         for s in reversed(range(SECTIONS)):
             rows = span(part)
             c = copy(gs.at[s, rows, :], gp.at[s, rows, :], partner(s))
-            if part is PARTS[0]:
+            if s not in joined:
                 fac_copies[s].wait_recv()
                 mp[s] = spread(fac_p[s])
+                joined.append(s)
             yield
             c.wait_recv()
             for i in part:
@@ -381,7 +414,11 @@
         put(fgrad.at[s], fgrad_out.at[s])
         yield
 
-    chains = {"G": gather(), "S": setup(), "R": scatter()}
+    chains = {"G": gather(), "GD": gather_dots(), "S": setup(), "R": scatter()}
+    for g in range(GROUPS):
+        for h, name in enumerate("AB"):
+            chains[f"G{name}{g}"] = gather_group(h, g)
+            chains[f"R{name}{g}"] = scatter_group(h, g)
     for n, part in enumerate(PARTS):
         chains[f"F{n}"] = forward(part)
         chains[f"B{n}"] = backward(part)
@@ -399,13 +436,13 @@
         c.wait()
 
 
-COPIES = 3 + 6 + 12 + 6 + 12 * len(PARTS) + 12 + 6 + 3 + 18
-STORES = 1 + len(PARTS) + SECTIONS
+COPIES = 3 + 6 + 18 + 12 * len(PARTS) + 2 * GROUPS * 21
+STORES = 2 * GROUPS + len(PARTS) + SECTIONS
 
 
 def body(hidden, weight, factors, cotangent):
     anywhere = pl.BlockSpec(memory_space=pl.ANY)
-    part = (SIDE, QUART, BLOCK)
+    part = (SIDE, CHUNK // GROUPS // 2, BLOCK)
     acts = (SECTIONS, WIDTH, ROWS)
     scratch = [
         ((SIDE * SIDE, WIDTH, BLOCK), BF16),
@@ -429,13 +466,10 @@
         ((SECTIONS, 2 * HALF, WIDTH), BF16),
         ((SECTIONS, 2 * HALF, WIDTH), F32),
         ((WIDTH, ROWS), F32),
-        ((2,) + part, BF16),
-        ((2, 2) + part, BF16),
-        ((2,) + part, BF16),
-        ((2, 2) + part, BF16),
-        ((3, CHUNK, BLOCK), BF16),
-        ((3, CHUNK, BLOCK), BF16),
-        ((3, ROWS, COL), BF16),
+        ((2, GROUPS, 2) + part, BF16),
+        ((2, GROUPS, 2, 2) + part, BF16),
+        ((2, GROUPS, 3, CHUNK // GROUPS, BLOCK), BF16),
+        ((2, GROUPS, 3, CHUNK // GROUPS, COL), BF16),
         ((ROWS, COL), BF16),
         ((WIDTH, ROWS), BF16),
         ((SECTIONS, LANES, 2 * HALF, 2 * HALF), F32),

time: 128 us -> 109 us (0.85)
  Pallas kernels: 121 us -> 102 us
    pallas_call x1, Pallas kernels: 121 us -> 102 us  [body(): pl.pallas_call(kernel, out_shape=(jax.ShapeDtypeStruct((ROWS, COL), BF16)...]
where the time goes in v3:
time: 109 us
  Pallas kernels  102 us (94%)
  local copies, waits for them, and re-layouts  5.68 us (5%)
    pallas_call x1, Pallas kernels, body(): pl.pallas_call(kernel, out_shape=(jax.ShapeDtypeStruct((ROWS, COL), BF16)...  102 us
    unnamed x3, local copies, waits for them, and re-layouts  5.68 us

profile of v3, /device:TPU:1, one launch (start us, length us, event | category | flops | bytes accessed | tf_op | source)
XLA Modules:
  0.0 108.6 jit_solution(4732734867443035834)
XLA Ops:
  0.6 102.3 %butterfly.1 = (bf16[256,128]{1,0:T(8,128)(2,1)}, bf16[448,256]{1,0:T(8,128)(2,1)}, f32[6,7,64,64]{3,2,1,0:T(8,128)}) custom-call(bf16[448,256]{1,0:T(8,128)(2,1)} %bitcast.3, bf16[448,8192]{1,0:T(8,128)(2,1)} %w_hbm.1, bf16[6,7,64,64]{3,2,1,0:T(8,128)(2,1)} %fac_hbm.1, bf16[256,128]{1,0:T(8,128)(2,1)} %cot_hbm.1), custom_call_target="tpu_custom_call" | custom-call | tf_op jit(solution)/shard_map/butterfly/pallas_call | solution.py:477
  103.0 1.5 %copy.10 = bf16[256,128]{1,0:T(8,128)(2,1)} copy(bf16[256,128]{1,0:T(8,128)(2,1)} %get-tuple-element.12) | data formatting | bytes 131072
  104.4 1.6 %copy.11 = bf16[256,448]{0,1:T(8,128)(2,1)} copy(bf16[256,448]{0,1:T(8,128)(2,1)} %bitcast.2) | data formatting | bytes 458752
  106.1 2.6 %copy.12 = f32[6,7,64,64]{3,2,1,0:T(8,128)} copy(f32[6,7,64,64]{3,2,1,0:T(8,128)} %get-tuple-element.14) | data formatting | bytes 1376256

commit v4 on v2

--- a/solution.py
+++ b/solution.py
@@ -17,17 +17,30 @@
 SIDE = 4
 COL = 128
 BLOCK = SIDE * COL
-CHUNK = 128
-QUART = 64
+HALVES = 2
+TOKENS = ROWS // HALVES
+GROUP = TOKENS // 2
+PIECE = GROUP // 2
 TILES = ((0, 128), (128, 128), (256, 128), (384, 64))
-PARTS = ((0, 1), (2, 3))
+SPLIT = ((0,), (1,), (2, 3))
+PARTS = tuple((tiles, half) for half in range(HALVES) for tiles in SPLIT)
+GROUPS = tuple((half, first) for half in range(HALVES) for first in (0, 1))
 
 SCHEDULE = (
-    ("G", "F0", "F1", "S", "F0", "F1", "G", "F0", "F1", "G", "F0", "F1", "G", "F0", "F1"),
-    ("F0", "F1", "G", "G", "B0", "B1", "F0", "F1", "R"),
-    ("D5", "B0", "B1", "D4", "D5", "R", "B0", "B1", "D3", "D4", "D5", "R"),
-    ("B0", "B1", "D2", "D3", "D4", "R", "B0", "B1", "D1", "D2", "D3", "R"),
-    ("B0", "B1", "D0", "D1", "D2", "D0", "D1", "B0", "B1", "D0"),
+    ("G0", "F0", "G1", "G2", "S", "G0", "F2", "G1", "G3", "F5", "G2", "F0"),
+    ("G0", "G1", "F0", "G3", "F3", "F2", "G1", "F5", "F1", "F2", "F4", "G0"),
+    ("G2", "G0", "F4", "G1", "G3", "F3", "N0", "G1", "F2", "F0", "F1", "G2"),
+    ("G0", "F4", "N0", "B2", "G2", "G3", "G3", "B1", "B0", "F1", "F2", "F0"),
+    ("N1", "B1", "B0", "G3", "G2", "F3", "F5", "B2", "F1", "F2", "N1", "B4"),
+    ("B3", "B1", "B5", "F4", "F5", "F0", "F3", "B2", "B4", "B1", "B0", "B3"),
+    ("F1", "B5", "F0", "F5", "B4", "F2", "B3", "B2", "F1", "B5", "F3", "F4"),
+    ("B3", "B4", "B0", "F5", "F1", "R0", "B1", "B2", "B5", "F3", "F4", "R0"),
+    ("R0", "D2", "R0", "B0", "D3", "B1", "B5", "F5", "B4", "F4", "Q1", "Q0"),
+    ("F3", "B3", "R1", "R1", "D2", "R1", "D4", "B5", "D5", "D3", "R1", "B2"),
+    ("D5", "B4", "B3", "B0", "Q2", "D4", "B5", "D1", "Q3", "D0", "Q1", "D0"),
+    ("Q0", "D3", "D2", "Q3", "Q2", "D1", "Q1", "D2", "Q0", "D4", "B3", "D0"),
+    ("Q3", "D4", "D5", "Q1", "D1", "D3", "Q2", "D5", "B4", "B0", "Q3", "B2"),
+    ("D1", "B1", "Q0", "Q2"),
 )
 
 
@@ -41,7 +54,7 @@
 def kernel(
     hid, w_hbm, fac_hbm, cot_hbm, proj_out, hgrad_out, fgrad_out,
     wv, cotv, facv, cotg, par, xs, xp, gs, gp, fac_t, fac_p, ma, mat, mbt, mp,
-    fg, fg_core, fg_half, fg_far, fg_all, acc, ra1, ra2, rb1, rb2, sa, sb, zr,
+    fg, fg_core, fg_half, fg_far, fg_all, acc, buf1, buf2, buf3, zr,
     proj, hgrad, fgrad, in_sem, out_sem, send, recv,
 ):
     dp = lax.axis_index("dp")
@@ -120,9 +133,18 @@
         pl.semaphore_signal(barrier, inc=1, device_id=dev, device_id_type=MESH)
     pl.semaphore_wait(barrier, len(peers))
 
-    half_a, half_b = pl.ds(0, CHUNK), pl.ds(CHUNK, CHUNK)
-    rows_a = (pl.ds(0, QUART), pl.ds(QUART, QUART))
-    rows_b = (pl.ds(CHUNK, QUART), pl.ds(CHUNK + QUART, QUART))
+    def start_of(i):
+        half, first = GROUPS[i]
+        return TOKENS * half + GROUP * first
+
+    def group(i):
+        return pl.ds(start_of(i), GROUP)
+
+    def piece(i, p):
+        return pl.ds(start_of(i) + PIECE * p, PIECE)
+
+    def tokens(half):
+        return pl.ds(TOKENS * half, TOKENS)
 
     def gather_phase(view, i, dev):
         r1 = copy(view(i, 0), view(i, 0), dev(1))
@@ -143,10 +165,10 @@
         far2.wait_recv()
         yield
 
-    def grad_dots(n, place):
+    def grad_dots(half, n, place):
         def step(k, carry):
             yy, xx = place(k)
-            acc[...] += dot(wv[yy * SIDE + xx], cotg[yy, xx], NT)
+            acc[half] += dot(wv[yy * SIDE + xx], cotg[yy, xx, tokens(half), :], NT)
             return carry
 
         lax.fori_loop(0, n, step, 0)
@@ -154,42 +176,49 @@
     def columns(zz):
         return pl.ds(pl.multiple_of(zz * COL, COL), COL)
 
-    def gather():
-        cot_copy.wait()
-        copies = [copy(cotv, cotg.at[y, x, :, columns(z)], z_dev(k)) for k in (1, 2, 3)]
-        cotg[y, x, :, columns(z)] = cotv[...]
-        acc[...] = jnp.zeros_like(acc)
+    loaded = []
+
+    def once(c):
+        if all(c is not d for d in loaded):
+            c.wait()
+            loaded.append(c)
+
+    def gather(i):
+        once(cot_copy)
+        first = GROUPS[i][1]
+        dev, dev2, n = ((x_dev, y_dev, y), (y_dev, x_dev, x))[first]
+        rows = group(i)
+        mine = cotg.at[y, x, rows, columns(z)]
+        copies = [copy(cotv.at[rows, :], mine, z_dev(k)) for k in (1, 2, 3)]
+        mine[...] = cotv[rows, :]
         yield
         for c in copies:
             c.wait_recv()
-        here_a, here_b = cotg.at[y, x, half_a, :], cotg.at[y, x, half_b, :]
-        copies = []
-        for k in (1, 3, 2):
-            copies.append(copy(here_a, here_a, x_dev(k)))
-            copies.append(copy(here_b, here_b, y_dev(k)))
+        here = cotg.at[y, x, rows, :]
+        copies = [copy(here, here, dev(k)) for k in (1, 3, 2)]
         yield
         for c in copies:
             c.wait_recv()
-        pa = gather_phase(lambda i, h: cotg.at[i, :, rows_a[h], :], y, y_dev)
-        pb = gather_phase(lambda i, h: cotg.at[:, i, rows_b[h], :], x, x_dev)
-        next(pa), next(pb)
-        yield
-        next(pa), next(pb)
-        yield
-        next(pa), next(pb)
+        if first == 0:
+            yield from gather_phase(lambda j, p: cotg.at[j, :, piece(i, p), :], n, dev2)
+        else:
+            yield from gather_phase(lambda j, p: cotg.at[:, j, piece(i, p), :], n, dev2)
+
+    def gather_dots(half):
         for c in w_copies:
-            c.wait()
-        grad_dots(9, lambda k: (ring(y, 3 + lax.div(k, 3)), ring(x, 3 + lax.rem(k, 3))))
-        yield
-        next(pa), next(pb)
+            once(c)
+        acc[half] = jnp.zeros((WIDTH, TOKENS), F32)
+        grad_dots(half, 9, lambda k: (ring(y, 3 + lax.div(k, 3)), ring(x, 3 + lax.rem(k, 3))))
+        yield
         grad_dots(
+            half,
             7,
             lambda k: (
                 ring(y, jnp.where(k < 4, 2, k - 1)),
                 ring(x, jnp.where(k < 4, k, 2)),
             ),
         )
-        gs[SECTIONS - 1] = acc[...].astype(BF16)
+        gs[SECTIONS - 1, :, tokens(half)] = acc[half].astype(BF16)
         yield
 
     diag = (
@@ -219,35 +248,32 @@
             turned(mbt.at[s], spread(fac_t[s, other_rows(s), :]))
         yield
 
-    def span(part):
-        lo = TILES[part[0]][0]
-        return pl.ds(lo, TILES[part[-1]][0] + TILES[part[-1]][1] - lo)
-
-    def forward(part):
-        if part is PARTS[0]:
-            hid_copy.wait()
+    def span(tiles):
+        lo = TILES[tiles[0]][0]
+        return pl.ds(lo, TILES[tiles[-1]][0] + TILES[tiles[-1]][1] - lo)
+
+    def forward(tiles, half):
+        once(hid_copy)
+        rows, cols = span(tiles), tokens(half)
         for s in range(SECTIONS):
-            rows = span(part)
-            c = copy(xs.at[s, rows, :], xp.at[s, rows, :], partner(s))
-            yield
-            c.wait_recv()
-            for i in part:
+            c = copy(xs.at[s, rows, cols], xp.at[s, rows, cols], partner(s))
+            yield
+            c.wait_recv()
+            for i in tiles:
                 lo, w = TILES[i]
-                own = xs[s, lo : lo + w, :]
+                own = xs[s, lo : lo + w, cols]
                 mix = dot(mat[s, lo : lo + w, 0:w], own)
-                mix += dot(mbt[s, lo : lo + w, 0:w], xp[s, lo : lo + w, :])
-                xs[s + 1, lo : lo + w, :] = (own.astype(F32) + mix).astype(BF16)
-        yield
-
-    def proj_dots(n, place):
+                mix += dot(mbt[s, lo : lo + w, 0:w], xp[s, lo : lo + w, cols])
+                xs[s + 1, lo : lo + w, cols] = (own.astype(F32) + mix).astype(BF16)
+        yield
+
+    def proj_dots(half, left, n, place):
         def step(k, carry):
             yy, xx = place(k)
-            par[yy, xx] = dot(proj_in[0], wv[yy * SIDE + xx]).astype(BF16)
+            par[yy, xx, tokens(half), :] = dot(left, wv[yy * SIDE + xx]).astype(BF16)
             return carry
 
         lax.fori_loop(0, n, step, 0)
-
-    proj_in = [None]
 
     def add_to(ref, *others):
         total = ref[...].astype(F32)
@@ -255,86 +281,108 @@
             total += o[...].astype(F32)
         ref[...] = total.astype(BF16)
 
-    def scatter_phase(view, i, buf1, buf2, dev):
-        p1, p2, m1 = ring(i, 1), ring(i, 2), ring(i, 3)
-        a = copy(view(p2, 0), buf1.at[0], dev(1))
-        b = copy(view(p2, 1), buf1.at[1], dev(3))
-        yield
-        c = copy(view(p1, 1), buf2.at[0, 1], dev(1))
-        d = copy(view(m1, 0), buf2.at[1, 0], dev(3))
-        yield
+    def sum_view(i):
+        if GROUPS[i][1] == 0:
+            return lambda j, p: par.at[j, :, piece(i, p), :]
+        return lambda j, p: par.at[:, j, piece(i, p), :]
+
+    early = {i: [] for i in range(len(GROUPS))}
+
+    def send_far(i):
+        n, dev = ((y, y_dev), (x, x_dev))[GROUPS[i][1]]
+        view = sum_view(i)
+        early[i].append(copy(view(ring(n, 2), 0), buf1.at[i, 0], dev(1)))
+        early[i].append(copy(view(ring(n, 2), 1), buf1.at[i, 1], dev(3)))
+
+    def send_near(i):
+        n, dev = ((y, y_dev), (x, x_dev))[GROUPS[i][1]]
+        view = sum_view(i)
+        early[i].append(copy(view(ring(n, 1), 1), buf2.at[i, 0, 1], dev(1)))
+        early[i].append(copy(view(ring(n, 3), 0), buf2.at[i, 1, 0], dev(3)))
+
+    def scatter(half):
+        for c in w_copies:
+            once(c)
+        left = xs[SECTIONS, :, tokens(half)].T
+        a, b = GROUPS.index((half, 0)), GROUPS.index((half, 1))
+        proj_dots(half, left, 4, lambda k: (ring(y, 2), ring(x, k)))
+        send_far(a)
+        yield
+        proj_dots(half, left, 3, lambda k: (ring(y, 3 + k), ring(x, 2)))
+        send_far(b)
+        yield
+        proj_dots(
+            half, left, 6,
+            lambda k: (ring(y, 1 + 2 * lax.div(k, 3)), ring(x, 3 + lax.rem(k, 3))),
+        )
+        send_near(a)
+        yield
+        proj_dots(half, left, 3, lambda k: (y, ring(x, 3 + k)))
+        send_near(b)
+        yield
+
+    def scatter_group(i):
+        view, rows = sum_view(i), group(i)
+        first = GROUPS[i][1]
+        n, dev, dev2 = ((y, y_dev, x_dev), (x, x_dev, y_dev))[first]
+        a, b, c, d = early[i]
         a.wait_recv()
-        add_to(view(p1, 0), buf1.at[0])
-        e = copy(view(p1, 0), buf2.at[0, 0], dev(1))
+        add_to(view(ring(n, 1), 0), buf1.at[i, 0])
+        e = copy(view(ring(n, 1), 0), buf2.at[i, 0, 0], dev(1))
         b.wait_recv()
-        add_to(view(m1, 1), buf1.at[1])
-        f = copy(view(m1, 1), buf2.at[1, 1], dev(3))
+        add_to(view(ring(n, 3), 1), buf1.at[i, 1])
+        f = copy(view(ring(n, 3), 1), buf2.at[i, 1, 1], dev(3))
         yield
         c.wait_recv()
         f.wait_recv()
-        add_to(view(i, 1), buf2.at[0, 1], buf2.at[1, 1])
+        add_to(view(n, 1), buf2.at[i, 0, 1], buf2.at[i, 1, 1])
         d.wait_recv()
         e.wait_recv()
-        add_to(view(i, 0), buf2.at[0, 0], buf2.at[1, 0])
-        yield
-
-    def scatter():
-        pa = scatter_phase(lambda i, h: par.at[i, :, rows_a[h], :], y, ra1, ra2, y_dev)
-        pb = scatter_phase(lambda i, h: par.at[:, i, rows_b[h], :], x, rb1, rb2, x_dev)
-        proj_in[0] = xs[SECTIONS].T
-        proj_dots(4, lambda k: (ring(y, 2), ring(x, k)))
-        next(pa)
-        proj_dots(3, lambda k: (ring(y, 3 + k), ring(x, 2)))
-        next(pb)
-        proj_dots(6, lambda k: (ring(y, 1 + 2 * lax.div(k, 3)), ring(x, 3 + lax.rem(k, 3))))
-        next(pa)
-        proj_dots(3, lambda k: (y, ring(x, 3 + k)))
-        next(pb)
-        yield
-        next(pa), next(pb)
-        yield
-        next(pa), next(pb)
+        add_to(view(n, 0), buf2.at[i, 0, 0], buf2.at[i, 1, 0])
         copies = []
         for k in (2, 1, 3):
-            copies.append(copy(par.at[y, ring(x, k), half_a, :], sa.at[k - 1], x_dev(k)))
-            copies.append(copy(par.at[ring(y, k), x, half_b, :], sb.at[k - 1], y_dev(k)))
+            src = par.at[y, ring(x, k), rows, :] if first == 0 else par.at[ring(y, k), x, rows, :]
+            copies.append(copy(src, buf3.at[i, k - 1], dev2(k)))
         yield
         for c in copies:
             c.wait_recv()
-        add_to(par.at[y, x, half_a, :], sa.at[0], sa.at[1], sa.at[2])
-        add_to(par.at[y, x, half_b, :], sb.at[0], sb.at[1], sb.at[2])
+        add_to(par.at[y, x, rows, :], *[buf3.at[i, k] for k in range(3)])
         copies = [
-            copy(par.at[y, x, :, columns(ring(z, k))], zr.at[k - 1], z_dev(k)) for k in (1, 2, 3)
+            copy(par.at[y, x, rows, columns(ring(z, k))], zr.at[i, k - 1], z_dev(k))
+            for k in (1, 2, 3)
         ]
         yield
-        total = par[y, x, :, columns(z)].astype(F32)
+        total = par[y, x, rows, columns(z)].astype(F32)
         for k in (1, 2, 3):
             copies[k - 1].wait_recv()
-            total += zr[k - 1].astype(F32)
-        proj[...] = total.astype(BF16)
-        put(proj, proj_out)
-        yield
-
-    def backward(part):
+            total += zr[i, k - 1].astype(F32)
+        proj[rows, :] = total.astype(BF16)
+        put(proj.at[rows, :], proj_out.at[rows, :])
+        yield
+
+    joined = []
+
+    def backward(tiles, half):
+        rows, cols = span(tiles), tokens(half)
         for s in reversed(range(SECTIONS)):
-            rows = span(part)
-            c = copy(gs.at[s, rows, :], gp.at[s, rows, :], partner(s))
-            if part is PARTS[0]:
+            c = copy(gs.at[s, rows, cols], gp.at[s, rows, cols], partner(s))
+            if s not in joined:
                 fac_copies[s].wait_recv()
                 mp[s] = spread(fac_p[s])
-            yield
-            c.wait_recv()
-            for i in part:
+                joined.append(s)
+            yield
+            c.wait_recv()
+            for i in tiles:
                 lo, w = TILES[i]
-                own = gs[s, lo : lo + w, :]
+                own = gs[s, lo : lo + w, cols]
                 back = dot(ma[s, 0:w, lo : lo + w], own)
-                back += dot(mp[s, 0:w, lo : lo + w], gp[s, lo : lo + w, :])
+                back += dot(mp[s, 0:w, lo : lo + w], gp[s, lo : lo + w, cols])
                 new = (own.astype(F32) + back).astype(BF16)
                 if s == 0:
-                    hgrad[lo : lo + w, :] = new
+                    hgrad[lo : lo + w, cols] = new
                 else:
-                    gs[s - 1, lo : lo + w, :] = new
-        put(hgrad.at[rows, :], hgrad_out.at[rows, :])
+                    gs[s - 1, lo : lo + w, cols] = new
+        put(hgrad.at[rows, cols], hgrad_out.at[rows, cols])
         yield
 
     keep = pl.ds(pl.multiple_of(HALF * core, HALF), HALF)
@@ -381,10 +429,16 @@
         put(fgrad.at[s], fgrad_out.at[s])
         yield
 
-    chains = {"G": gather(), "S": setup(), "R": scatter()}
-    for n, part in enumerate(PARTS):
-        chains[f"F{n}"] = forward(part)
-        chains[f"B{n}"] = backward(part)
+    chains = {"S": setup()}
+    for half in range(HALVES):
+        chains[f"N{half}"] = gather_dots(half)
+        chains[f"R{half}"] = scatter(half)
+    for i in range(len(GROUPS)):
+        chains[f"G{i}"] = gather(i)
+        chains[f"Q{i}"] = scatter_group(i)
+    for i, part in enumerate(PARTS):
+        chains[f"F{i}"] = forward(*part)
+        chains[f"B{i}"] = backward(*part)
     for s in range(SECTIONS):
         chains[f"D{s}"] = factor(s)
     for name in sum(SCHEDULE, ()):
@@ -399,13 +453,18 @@
         c.wait()
 
 
-COPIES = 3 + 6 + 12 + 6 + 12 * len(PARTS) + 12 + 6 + 3 + 18
-STORES = 1 + len(PARTS) + SECTIONS
+COPIES = 6 + 18 + 12 * len(PARTS) + 24 * len(GROUPS)
+STORES = len(GROUPS) + len(PARTS) + SECTIONS
+
+
+def hand_on(*refs):
+    for i in range(3):
+        refs[3 + i][...] = refs[i][...]
 
 
 def body(hidden, weight, factors, cotangent):
     anywhere = pl.BlockSpec(memory_space=pl.ANY)
-    part = (SIDE, QUART, BLOCK)
+    groups, part = len(GROUPS), (SIDE, PIECE, BLOCK)
     acts = (SECTIONS, WIDTH, ROWS)
     scratch = [
         ((SIDE * SIDE, WIDTH, BLOCK), BF16),
@@ -428,14 +487,11 @@
         ((2 * HALF, WIDTH), BF16),
         ((SECTIONS, 2 * HALF, WIDTH), BF16),
         ((SECTIONS, 2 * HALF, WIDTH), F32),
-        ((WIDTH, ROWS), F32),
-        ((2,) + part, BF16),
-        ((2, 2) + part, BF16),
-        ((2,) + part, BF16),
-        ((2, 2) + part, BF16),
-        ((3, CHUNK, BLOCK), BF16),
-        ((3, CHUNK, BLOCK), BF16),
-        ((3, ROWS, COL), BF16),
+        ((HALVES, WIDTH, TOKENS), F32),
+        ((groups, 2) + part, BF16),
+        ((groups, 2, 2) + part, BF16),
+        ((groups, 3, GROUP, BLOCK), BF16),
+        ((groups, 3, GROUP, COL), BF16),
         ((ROWS, COL), BF16),
         ((WIDTH, ROWS), BF16),
         ((SECTIONS, LANES, 2 * HALF, 2 * HALF), F32),
@@ -461,6 +517,14 @@
         ),
         name="butterfly",
     )(hidden.T, weight, factors, cotangent)
+    outs = (proj, hgrad, fgrad)
+    proj, hgrad, fgrad = pl.pallas_call(
+        hand_on,
+        out_shape=tuple(jax.ShapeDtypeStruct(o.shape, o.dtype) for o in outs),
+        in_specs=[pl.BlockSpec(memory_space=pltpu.VMEM)] * 3,
+        out_specs=(pl.BlockSpec(memory_space=pltpu.VMEM),) * 3,
+        name="hand_on",
+    )(*outs)
     return proj, hgrad.T, fgrad
 
 

time: 128 us -> 102 us (0.80)
  Pallas kernels: 121 us -> 101 us
  local copies, waits for them, and re-layouts: 5.68 us -> 0 us
    pallas_call x1, Pallas kernels: 121 us -> 98.4 us  [body(): pl.pallas_call(kernel, out_shape=(jax.ShapeDtypeStruct((ROWS, COL), BF16)...]
    unnamed x3 -> x0, local copies, waits for them, and re-layouts: 5.68 us -> none
    pallas_call x0 -> x1, Pallas kernels: none -> 2.7 us  [body(): pl.pallas_call(hand_on, out_shape=tuple((jax.ShapeDtypeStruct(o.shape, o....]
where the time goes in v4:
time: 102 us
  Pallas kernels  101 us (99%)
    pallas_call x1, Pallas kernels, body(): pl.pallas_call(kernel, out_shape=(jax.ShapeDtypeStruct((ROWS, COL), BF16)...  98.4 us
    pallas_call x1, Pallas kernels, body(): pl.pallas_call(hand_on, out_shape=tuple((jax.ShapeDtypeStruct(o.shape, o....  2.7 us

profile of v4, /device:TPU:1, one launch (start us, length us, event | category | flops | bytes accessed | tf_op | source)
XLA Modules:
  0.0 101.8 jit_solution(6738462541027540235)
XLA Ops:
  0.6 98.4 %butterfly.1 = (bf16[256,128]{1,0:T(8,128)(2,1)}, bf16[448,256]{1,0:T(8,128)(2,1)}, f32[6,7,64,64]{3,2,1,0:T(8,128)}) custom-call(bf16[448,256]{1,0:T(8,128)(2,1)} %bitcast.2, bf16[448,8192]{1,0:T(8,128)(2,1)} %w_hbm.1, bf16[6,7,64,64]{3,2,1,0:T(8,128)(2,1)} %fac_hbm.1, bf16[256,128]{1,0:T(8,128)(2,1)} %cot_hbm.1), custom_call_target="tpu_custom_call" | custom-call | tf_op jit(solution)/shard_map/butterfly/pallas_call | solution.py:499
  99.1 2.7 %hand_on.1 = (bf16[256,128]{1,0:T(8,128)(2,1)}, bf16[448,256]{1,0:T(8,128)(2,1)}, f32[6,7,64,64]{3,2,1,0:T(8,128)}) custom-call(bf16[256,128]{1,0:T(8,128)(2,1)} %get-tuple-element.9.refs_0_, bf16[448,256]{1,0:T(8,128)(2,1)} %get-tuple-element.10.refs_1_, f32[6,7,64,64]{3,2,1,0:T(8,128)} %get-tuple-element.11.refs_2_), custom_call_target="tpu_custom_call" | custom-call | tf_op jit(solution)/shard_map/hand_on/pallas_call | solution.py:521

commit v5 on v4

--- a/solution.py
+++ b/solution.py
@@ -20,27 +20,29 @@
 HALVES = 2
 TOKENS = ROWS // HALVES
 GROUP = TOKENS // 2
-PIECE = GROUP // 2
+SLACK = GROUP // 2
 TILES = ((0, 128), (128, 128), (256, 128), (384, 64))
 SPLIT = ((0,), (1,), (2, 3))
 PARTS = tuple((tiles, half) for half in range(HALVES) for tiles in SPLIT)
 GROUPS = tuple((half, first) for half in range(HALVES) for first in (0, 1))
 
+BATCHES = ((5, 4, 3), (2, 1), (0,))
+
 SCHEDULE = (
-    ("G0", "F0", "G1", "G2", "S", "G0", "F2", "G1", "G3", "F5", "G2", "F0"),
-    ("G0", "G1", "F0", "G3", "F3", "F2", "G1", "F5", "F1", "F2", "F4", "G0"),
-    ("G2", "G0", "F4", "G1", "G3", "F3", "N0", "G1", "F2", "F0", "F1", "G2"),
-    ("G0", "F4", "N0", "B2", "G2", "G3", "G3", "B1", "B0", "F1", "F2", "F0"),
-    ("N1", "B1", "B0", "G3", "G2", "F3", "F5", "B2", "F1", "F2", "N1", "B4"),
-    ("B3", "B1", "B5", "F4", "F5", "F0", "F3", "B2", "B4", "B1", "B0", "B3"),
-    ("F1", "B5", "F0", "F5", "B4", "F2", "B3", "B2", "F1", "B5", "F3", "F4"),
-    ("B3", "B4", "B0", "F5", "F1", "R0", "B1", "B2", "B5", "F3", "F4", "R0"),
-    ("R0", "D2", "R0", "B0", "D3", "B1", "B5", "F5", "B4", "F4", "Q1", "Q0"),
-    ("F3", "B3", "R1", "R1", "D2", "R1", "D4", "B5", "D5", "D3", "R1", "B2"),
-    ("D5", "B4", "B3", "B0", "Q2", "D4", "B5", "D1", "Q3", "D0", "Q1", "D0"),
-    ("Q0", "D3", "D2", "Q3", "Q2", "D1", "Q1", "D2", "Q0", "D4", "B3", "D0"),
-    ("Q3", "D4", "D5", "Q1", "D1", "D3", "Q2", "D5", "B4", "B0", "Q3", "B2"),
-    ("D1", "B1", "Q0", "Q2"),
+    ("F2", "G2", "G3", "G0", "G1", "F2", "S", "G2", "G3", "G0", "G1", "F1"),
+    ("F2", "G2", "G3", "F4", "F0", "F5", "F0", "F5", "F2", "G2", "F1", "G3"),
+    ("G0", "F0", "F3", "G1", "G3", "G2", "N1", "F2", "G3", "F0", "G2", "N1"),
+    ("B3", "F1", "B5", "H", "F4", "G1", "G0", "F3", "B4", "G0", "F2", "G1"),
+    ("F5", "N0", "F1", "B3", "F0", "B5", "F3", "H", "G0", "G1", "N0", "B2"),
+    ("F4", "F5", "B0", "F1", "B1", "F3", "F2", "B3", "F0", "B4", "F4", "H"),
+    ("B5", "F1", "B2", "F5", "B4", "B0", "B3", "B1", "F0", "F3", "F4", "B5"),
+    ("F1", "B2", "R0", "H", "B4", "B0", "B1", "F5", "E3", "B3", "B5", "R0"),
+    ("F4", "F3", "R0", "B0", "E4", "B2", "B1", "H", "B4", "R0", "F5", "F4"),
+    ("F3", "R1", "R1", "B2", "R1", "B0", "Q1", "B1", "B3", "E5", "B5", "D0"),
+    ("Q2", "R1", "B4", "B0", "Q0", "D0", "B2", "Q3", "B1", "E1", "E0", "B3"),
+    ("D2", "E2", "D1", "Q1", "D1", "D2", "Q2", "Q3", "B1", "Q0", "D0", "B2"),
+    ("Q1", "Q2", "Q3", "B4", "Q0", "D1", "B0", "Q1", "B5", "D1", "D0", "Q2"),
+    ("Q3", "D2", "Q0"),
 )
 
 
@@ -55,7 +57,7 @@
     hid, w_hbm, fac_hbm, cot_hbm, proj_out, hgrad_out, fgrad_out,
     wv, cotv, facv, cotg, par, xs, xp, gs, gp, fac_t, fac_p, ma, mat, mbt, mp,
     fg, fg_core, fg_half, fg_far, fg_all, acc, buf1, buf2, buf3, zr,
-    proj, hgrad, fgrad, in_sem, out_sem, send, recv,
+    proj, hgrad, fgrad, in_sem, out_sem, word, send, recv,
 ):
     dp = lax.axis_index("dp")
     t = lax.axis_index("tensor")
@@ -127,10 +129,38 @@
         stored.append(c)
 
     peers = [f(k) for f in (z_dev, x_dev, y_dev) for k in (1, 2, 3)]
-    peers += [core_dev, far_dev, cross_dev]
+    run = lax.div(dp, 2) * SIDE + z
+
+    def run_dev(k):
+        to = lax.rem(run + k, 2 * SIDE)
+        return (lax.div(to, SIDE) * 2 + core, t - z + lax.rem(to, SIDE))
+
+    ends = [run_dev(1), run_dev(2 * SIDE - 1)]
+    peers += [core_dev] + ends
     barrier = pltpu.get_barrier_semaphore()
     for dev in peers:
         pl.semaphore_signal(barrier, inc=1, device_id=dev, device_id_type=MESH)
+    diag = (
+        lax.broadcasted_iota(jnp.int32, (COL, WIDTH), 0) // HALF
+        == lax.rem(lax.broadcasted_iota(jnp.int32, (COL, WIDTH), 1), COL) // HALF
+    )
+
+    def spread(part):
+        return jnp.where(diag, jnp.concatenate([part] * 4, axis=0), jnp.zeros((), BF16))
+
+    def turned(ref, full):
+        for lo, w in TILES:
+            ref[lo : lo + w, 0:w] = full[0:w, lo : lo + w].T
+
+    fac_copy.wait()
+    for s in range(SECTIONS):
+        fac_t[s] = jnp.concatenate([facv[s, j] for j in range(LANES)], axis=1)
+        own = spread(fac_t[s, own_rows(s), :])
+        ma[s] = own
+        turned(mat.at[s], own)
+        turned(mbt.at[s], spread(fac_t[s, other_rows(s), :]))
+    cot_copy.wait()
+    hid_copy.wait()
     pl.semaphore_wait(barrier, len(peers))
 
     def start_of(i):
@@ -140,23 +170,30 @@
     def group(i):
         return pl.ds(start_of(i), GROUP)
 
+    pieces = ((0, SLACK), (SLACK, GROUP - SLACK))
+
     def piece(i, p):
-        return pl.ds(start_of(i) + PIECE * p, PIECE)
+        return pl.ds(start_of(i) + pieces[p][0], pieces[p][1])
+
+    def bound(v):
+        return 1 + 2 * lax.rem(v, 2), 3 - 2 * lax.rem(v, 2)
 
     def tokens(half):
         return pl.ds(TOKENS * half, TOKENS)
 
     def gather_phase(view, i, dev):
-        r1 = copy(view(i, 0), view(i, 0), dev(1))
-        l2 = copy(view(i, 1), view(i, 1), dev(3))
-        r2 = copy(view(i, 1), view(i, 1), dev(1))
-        l1 = copy(view(i, 0), view(i, 0), dev(3))
-        yield
-        left, right = ring(i, 3), ring(i, 1)
+        near, other = bound(i)
+        r1 = copy(view(i, 0), view(i, 0), dev(near))
+        l2 = copy(view(i, 1), view(i, 1), dev(other))
+        r2 = copy(view(i, 1), view(i, 1), dev(near))
+        l1 = copy(view(i, 0), view(i, 0), dev(other))
+        yield
         r1.wait_recv()
-        far1 = copy(view(left, 0), view(left, 0), dev(1))
+        there = view(ring(i, near), 0)
+        far1 = copy(there, there, dev(other))
         l2.wait_recv()
-        far2 = copy(view(right, 1), view(right, 1), dev(3))
+        there = view(ring(i, other), 1)
+        far2 = copy(there, there, dev(near))
         yield
         r2.wait_recv()
         l1.wait_recv()
@@ -184,7 +221,6 @@
             loaded.append(c)
 
     def gather(i):
-        once(cot_copy)
         first = GROUPS[i][1]
         dev, dev2, n = ((x_dev, y_dev, y), (y_dev, x_dev, x))[first]
         rows = group(i)
@@ -221,31 +257,11 @@
         gs[SECTIONS - 1, :, tokens(half)] = acc[half].astype(BF16)
         yield
 
-    diag = (
-        lax.broadcasted_iota(jnp.int32, (COL, WIDTH), 0) // HALF
-        == lax.rem(lax.broadcasted_iota(jnp.int32, (COL, WIDTH), 1), COL) // HALF
-    )
-
-    def spread(part):
-        return jnp.where(diag, jnp.concatenate([part] * 4, axis=0), jnp.zeros((), BF16))
-
-    def turned(ref, full):
-        for lo, w in TILES:
-            ref[lo : lo + w, 0:w] = full[0:w, lo : lo + w].T
-
     fac_copies = [None] * SECTIONS
 
     def setup():
-        fac_copy.wait()
-        for s in range(SECTIONS):
-            fac_t[s] = jnp.concatenate([facv[s, j] for j in range(LANES)], axis=1)
         for s in reversed(range(SECTIONS)):
             fac_copies[s] = copy(fac_t.at[s, other_rows(s), :], fac_p.at[s], partner(s))
-        for s in range(SECTIONS):
-            own = spread(fac_t[s, own_rows(s), :])
-            ma[s] = own
-            turned(mat.at[s], own)
-            turned(mbt.at[s], spread(fac_t[s, other_rows(s), :]))
         yield
 
     def span(tiles):
@@ -253,7 +269,6 @@
         return pl.ds(lo, TILES[tiles[-1]][0] + TILES[tiles[-1]][1] - lo)
 
     def forward(tiles, half):
-        once(hid_copy)
         rows, cols = span(tiles), tokens(half)
         for s in range(SECTIONS):
             c = copy(xs.at[s, rows, cols], xp.at[s, rows, cols], partner(s))
@@ -288,17 +303,22 @@
 
     early = {i: [] for i in range(len(GROUPS))}
 
+    def landing(buf, p):
+        return buf.at[:, pl.ds(*pieces[p]), :]
+
     def send_far(i):
         n, dev = ((y, y_dev), (x, x_dev))[GROUPS[i][1]]
         view = sum_view(i)
-        early[i].append(copy(view(ring(n, 2), 0), buf1.at[i, 0], dev(1)))
-        early[i].append(copy(view(ring(n, 2), 1), buf1.at[i, 1], dev(3)))
+        near, other = bound(n)
+        early[i].append(copy(view(ring(n, 2), 0), landing(buf1.at[i], 0), dev(other)))
+        early[i].append(copy(view(ring(n, 2), 1), landing(buf1.at[i], 1), dev(near)))
 
     def send_near(i):
         n, dev = ((y, y_dev), (x, x_dev))[GROUPS[i][1]]
         view = sum_view(i)
-        early[i].append(copy(view(ring(n, 1), 1), buf2.at[i, 0, 1], dev(1)))
-        early[i].append(copy(view(ring(n, 3), 0), buf2.at[i, 1, 0], dev(3)))
+        near, other = bound(n)
+        early[i].append(copy(view(ring(n, near), 1), landing(buf2.at[i, 0], 1), dev(near)))
+        early[i].append(copy(view(ring(n, other), 0), landing(buf2.at[i, 1], 0), dev(other)))
 
     def scatter(half):
         for c in w_copies:
@@ -325,20 +345,21 @@
         view, rows = sum_view(i), group(i)
         first = GROUPS[i][1]
         n, dev, dev2 = ((y, y_dev, x_dev), (x, x_dev, y_dev))[first]
+        near, other = bound(n)
         a, b, c, d = early[i]
         a.wait_recv()
-        add_to(view(ring(n, 1), 0), buf1.at[i, 0])
-        e = copy(view(ring(n, 1), 0), buf2.at[i, 0, 0], dev(1))
+        add_to(view(ring(n, near), 0), landing(buf1.at[i], 0))
+        e = copy(view(ring(n, near), 0), landing(buf2.at[i, 0], 0), dev(near))
         b.wait_recv()
-        add_to(view(ring(n, 3), 1), buf1.at[i, 1])
-        f = copy(view(ring(n, 3), 1), buf2.at[i, 1, 1], dev(3))
+        add_to(view(ring(n, other), 1), landing(buf1.at[i], 1))
+        f = copy(view(ring(n, other), 1), landing(buf2.at[i, 1], 1), dev(other))
         yield
         c.wait_recv()
         f.wait_recv()
-        add_to(view(n, 1), buf2.at[i, 0, 1], buf2.at[i, 1, 1])
+        add_to(view(n, 1), landing(buf2.at[i, 0], 1), landing(buf2.at[i, 1], 1))
         d.wait_recv()
         e.wait_recv()
-        add_to(view(n, 0), buf2.at[i, 0, 0], buf2.at[i, 1, 0])
+        add_to(view(n, 0), landing(buf2.at[i, 0], 0), landing(buf2.at[i, 1], 0))
         copies = []
         for k in (2, 1, 3):
             src = par.at[y, ring(x, k), rows, :] if first == 0 else par.at[ring(y, k), x, rows, :]
@@ -397,39 +418,54 @@
                 for g in range(1, w // HALF):
                     total += full[g * HALF : (g + 1) * HALF]
                 fg[s, rows, lo : lo + w] = total
-        if s == 0:
-            a = copy(fg.at[s], fg_all.at[s], core_dev)
+        yield
+
+    def reduce(batch):
+        some = pl.ds(min(batch), len(batch))
+        if 0 in batch:
+            a = copy(fg.at[some], fg_all.at[some], core_dev)
             yield
             a.wait_recv()
-            chip = (fg[s] + fg_all[s]).astype(BF16)
-            fg_half[...] = chip
-            b = copy(fg_half.at[keep, :], fg_far.at[s, keep, :], far_dev)
-            c = copy(fg_half.at[keep, :], fg_far.at[s, keep, :], cross_dev)
+            chip = (fg[some] + fg_all[some]).astype(BF16)
+            fg_half[some] = chip
+            b = copy(fg_half.at[some, keep, :], fg_far.at[some, keep, :], far_dev)
+            c = copy(fg_half.at[some, keep, :], fg_far.at[some, keep, :], cross_dev)
             yield
             b.wait_recv()
             c.wait_recv()
-            total = chip.astype(F32) + fg_far[s].astype(F32)
+            total = chip.astype(F32) + fg_far[some].astype(F32)
         else:
-            a = copy(fg.at[s, give, :], fg_core.at[s], core_dev)
+            a = copy(fg.at[some, give, :], fg_core.at[some], core_dev)
             yield
             a.wait_recv()
-            chip = (fg[s, keep, :] + fg_core[s]).astype(BF16)
-            fg_far[s, give, :] = chip
-            b = copy(fg_far.at[s, give, :], fg_far.at[s, keep, :], far_dev)
+            chip = (fg[some, keep, :] + fg_core[some]).astype(BF16)
+            fg_half[some, keep, :] = chip
+            b = copy(fg_half.at[some, keep, :], fg_far.at[some, keep, :], far_dev)
             yield
             b.wait_recv()
-            fg_all[s, keep, :] = chip.astype(F32) + fg_far[s, keep, :].astype(F32)
-            c = copy(fg_all.at[s, keep, :], fg_all.at[s, keep, :], core_dev)
-            yield
-            c.wait_recv()
-            total = fg_all[s]
+            fg_all[some, keep, :] = chip.astype(F32) + fg_far[some, keep, :].astype(F32)
+            c = copy(fg_all.at[some, keep, :], fg_all.at[some, keep, :], core_dev)
+            yield
+            c.wait_recv()
+            total = fg_all[some]
         total = total * (1.0 / (4 * ROWS))
         for j in range(LANES):
-            fgrad[s, j] = total[:, 2 * HALF * j : 2 * HALF * (j + 1)]
-        put(fgrad.at[s], fgrad_out.at[s])
-        yield
-
-    chains = {"S": setup()}
+            fgrad[some, j] = total[:, :, 2 * HALF * j : 2 * HALF * (j + 1)]
+        put(fgrad.at[some], fgrad_out.at[some])
+        yield
+
+    def greet():
+        for r in range(3):
+            for dev in ends:
+                pl.semaphore_signal(word.at[r], inc=1, device_id=dev, device_id_type=MESH)
+            yield
+            pl.semaphore_wait(word.at[r], 2)
+        pl.semaphore_signal(word.at[3], inc=1, device_id=core_dev, device_id_type=MESH)
+        yield
+        pl.semaphore_wait(word.at[3], 1)
+        yield
+
+    chains = {"S": setup(), "H": greet()}
     for half in range(HALVES):
         chains[f"N{half}"] = gather_dots(half)
         chains[f"R{half}"] = scatter(half)
@@ -440,7 +476,9 @@
         chains[f"F{i}"] = forward(*part)
         chains[f"B{i}"] = backward(*part)
     for s in range(SECTIONS):
-        chains[f"D{s}"] = factor(s)
+        chains[f"E{s}"] = factor(s)
+    for i, batch in enumerate(BATCHES):
+        chains[f"D{i}"] = reduce(batch)
     for name in sum(SCHEDULE, ()):
         next(chains[name], None)
     for chain in chains.values():
@@ -453,8 +491,8 @@
         c.wait()
 
 
-COPIES = 6 + 18 + 12 * len(PARTS) + 24 * len(GROUPS)
-STORES = len(GROUPS) + len(PARTS) + SECTIONS
+COPIES = 6 + 12 * len(PARTS) + 24 * len(GROUPS) + 3 * len(BATCHES)
+STORES = len(GROUPS) + len(PARTS) + len(BATCHES)
 
 
 def hand_on(*refs):
@@ -464,7 +502,7 @@
 
 def body(hidden, weight, factors, cotangent):
     anywhere = pl.BlockSpec(memory_space=pl.ANY)
-    groups, part = len(GROUPS), (SIDE, PIECE, BLOCK)
+    groups, part = len(GROUPS), (SIDE, GROUP, BLOCK)
     acts = (SECTIONS, WIDTH, ROWS)
     scratch = [
         ((SIDE * SIDE, WIDTH, BLOCK), BF16),
@@ -484,12 +522,12 @@
         ((SECTIONS, COL, WIDTH), BF16),
         ((SECTIONS, 2 * HALF, WIDTH), F32),
         ((SECTIONS, HALF, WIDTH), F32),
-        ((2 * HALF, WIDTH), BF16),
+        ((SECTIONS, 2 * HALF, WIDTH), BF16),
         ((SECTIONS, 2 * HALF, WIDTH), BF16),
         ((SECTIONS, 2 * HALF, WIDTH), F32),
         ((HALVES, WIDTH, TOKENS), F32),
+        ((groups,) + part, BF16),
         ((groups, 2) + part, BF16),
-        ((groups, 2, 2) + part, BF16),
         ((groups, 3, GROUP, BLOCK), BF16),
         ((groups, 3, GROUP, COL), BF16),
         ((ROWS, COL), BF16),
@@ -509,6 +547,7 @@
         + [
             pltpu.SemaphoreType.DMA((3 + SIDE * SIDE,)),
             pltpu.SemaphoreType.DMA((STORES,)),
+            pltpu.SemaphoreType.REGULAR((4,)),
             pltpu.SemaphoreType.DMA((COPIES,)),
             pltpu.SemaphoreType.DMA((COPIES,)),
         ],

time: 102 us -> 97.2 us (0.953)
  Pallas kernels: 101 us -> 96.5 us
    pallas_call x1, Pallas kernels: 98.4 us -> 93.8 us  [body(): pl.pallas_call(kernel, out_shape=(jax.ShapeDtypeStruct((ROWS, COL), BF16)...]
where the time goes in v5:
time: 97.2 us; the launch traced here: 97.1 us
  Pallas kernels  96.5 us (99%)
    pallas_call x1, Pallas kernels, body(): pl.pallas_call(kernel, out_shape=(jax.ShapeDtypeStruct((ROWS, COL), BF16)...  93.8 us
    pallas_call x1, Pallas kernels, body(): pl.pallas_call(hand_on, out_shape=tuple((jax.ShapeDtypeStruct(o.shape, o....  2.7 us

profile of v5, /device:TPU:1, one launch (start us, length us, event | category | flops | bytes accessed | tf_op | source)
XLA Modules:
  0.0 97.1 jit_solution(1149525921712825141)
XLA Ops:
  0.6 93.8 %butterfly.1 = (bf16[256,128]{1,0:T(8,128)(2,1)}, bf16[448,256]{1,0:T(8,128)(2,1)}, f32[6,7,64,64]{3,2,1,0:T(8,128)}) custom-call(bf16[448,256]{1,0:T(8,128)(2,1)} %bitcast.2, bf16[448,8192]{1,0:T(8,128)(2,1)} %w_hbm.1, bf16[6,7,64,64]{3,2,1,0:T(8,128)(2,1)} %fac_hbm.1, bf16[256,128]{1,0:T(8,128)(2,1)} %cot_hbm.1), custom_call_target="tpu_custom_call" | custom-call | tf_op jit(solution)/shard_map/butterfly/pallas_call | solution.py:537
  94.4 2.7 %hand_on.1 = (bf16[256,128]{1,0:T(8,128)(2,1)}, bf16[448,256]{1,0:T(8,128)(2,1)}, f32[6,7,64,64]{3,2,1,0:T(8,128)}) custom-call(bf16[256,128]{1,0:T(8,128)(2,1)} %get-tuple-element.9.refs_0_, bf16[448,256]{1,0:T(8,128)(2,1)} %get-tuple-element.10.refs_1_, f32[6,7,64,64]{3,2,1,0:T(8,128)} %get-tuple-element.11.refs_2_), custom_call_target="tpu_custom_call" | custom-call | tf_op jit(solution)/shard_map/hand_on/pallas_call | solution.py:560

commit v6 on v5

--- a/solution.py
+++ b/solution.py
@@ -22,27 +22,24 @@
 GROUP = TOKENS // 2
 SLACK = GROUP // 2
 TILES = ((0, 128), (128, 128), (256, 128), (384, 64))
-SPLIT = ((0,), (1,), (2, 3))
+SPLIT = ((0, 1), (2, 3))
 PARTS = tuple((tiles, half) for half in range(HALVES) for tiles in SPLIT)
 GROUPS = tuple((half, first) for half in range(HALVES) for first in (0, 1))
 
 BATCHES = ((5, 4, 3), (2, 1), (0,))
 
 SCHEDULE = (
-    ("F2", "G2", "G3", "G0", "G1", "F2", "S", "G2", "G3", "G0", "G1", "F1"),
-    ("F2", "G2", "G3", "F4", "F0", "F5", "F0", "F5", "F2", "G2", "F1", "G3"),
-    ("G0", "F0", "F3", "G1", "G3", "G2", "N1", "F2", "G3", "F0", "G2", "N1"),
-    ("B3", "F1", "B5", "H", "F4", "G1", "G0", "F3", "B4", "G0", "F2", "G1"),
-    ("F5", "N0", "F1", "B3", "F0", "B5", "F3", "H", "G0", "G1", "N0", "B2"),
-    ("F4", "F5", "B0", "F1", "B1", "F3", "F2", "B3", "F0", "B4", "F4", "H"),
-    ("B5", "F1", "B2", "F5", "B4", "B0", "B3", "B1", "F0", "F3", "F4", "B5"),
-    ("F1", "B2", "R0", "H", "B4", "B0", "B1", "F5", "E3", "B3", "B5", "R0"),
-    ("F4", "F3", "R0", "B0", "E4", "B2", "B1", "H", "B4", "R0", "F5", "F4"),
-    ("F3", "R1", "R1", "B2", "R1", "B0", "Q1", "B1", "B3", "E5", "B5", "D0"),
-    ("Q2", "R1", "B4", "B0", "Q0", "D0", "B2", "Q3", "B1", "E1", "E0", "B3"),
-    ("D2", "E2", "D1", "Q1", "D1", "D2", "Q2", "Q3", "B1", "Q0", "D0", "B2"),
-    ("Q1", "Q2", "Q3", "B4", "Q0", "D1", "B0", "Q1", "B5", "D1", "D0", "Q2"),
-    ("Q3", "D2", "Q0"),
+    ("G3", "G2", "G1", "F2", "G0", "S", "G3", "F1", "G2", "G1", "G0", "G3"),
+    ("F1", "F0", "G2", "F3", "F0", "F1", "F3", "G3", "G2", "G0", "G3", "F1"),
+    ("F0", "G2", "G1", "N1", "G2", "G3", "N1", "B3", "H", "F2", "B2", "G0"),
+    ("F0", "F1", "G1", "B3", "F2", "G1", "F3", "G0", "B2", "H", "N0", "G0"),
+    ("F0", "F1", "B3", "G1", "N0", "B1", "B2", "F2", "B0", "F0", "H", "F3"),
+    ("B1", "B2", "B0", "F1", "B3", "F2", "F3", "F0", "B1", "R0", "B0", "H"),
+    ("R0", "B2", "B3", "F3", "F2", "B1", "R0", "B0", "R0", "Q0", "E3", "E4"),
+    ("H", "F3", "B2", "Q1", "B1", "F2", "R1", "R1", "B0", "R1", "R1", "B3"),
+    ("E5", "D0", "B1", "Q2", "D0", "Q3", "B0", "E0", "D2", "Q1", "B1", "D2"),
+    ("Q0", "B3", "E2", "E1", "D1", "Q2", "D1", "Q3", "B2", "D0", "Q1", "Q0"),
+    ("Q2", "Q3", "D2", "D1", "Q1", "B0", "D0", "D1", "Q0", "Q2", "Q3"),
 )
 
 
@@ -495,9 +492,18 @@
 STORES = len(GROUPS) + len(PARTS) + len(BATCHES)
 
 
-def hand_on(*refs):
-    for i in range(3):
-        refs[3 + i][...] = refs[i][...]
+def hand_on(proj, hgrad, fgrad, proj_out, hgrad_out, fgrad_out, pv, hv, fv, in_sem, out_sem):
+    moves = [(proj, pv, proj_out), (hgrad, hv, hgrad_out)]
+    moves += [(fgrad.at[s], fv.at[s], fgrad_out.at[s]) for s in range(SECTIONS)]
+    ins = [pltpu.make_async_copy(m[0], m[1], in_sem.at[i]) for i, m in enumerate(moves)]
+    outs = [pltpu.make_async_copy(m[1], m[2], out_sem.at[i]) for i, m in enumerate(moves)]
+    for c in ins:
+        c.start()
+    for i, o in zip(ins, outs):
+        i.wait()
+        o.start()
+    for c in outs:
+        c.wait()
 
 
 def body(hidden, weight, factors, cotangent):
@@ -560,8 +566,10 @@
     proj, hgrad, fgrad = pl.pallas_call(
         hand_on,
         out_shape=tuple(jax.ShapeDtypeStruct(o.shape, o.dtype) for o in outs),
-        in_specs=[pl.BlockSpec(memory_space=pltpu.VMEM)] * 3,
-        out_specs=(pl.BlockSpec(memory_space=pltpu.VMEM),) * 3,
+        in_specs=[anywhere] * 3,
+        out_specs=(anywhere,) * 3,
+        scratch_shapes=[pltpu.VMEM(o.shape, o.dtype) for o in outs]
+        + [pltpu.SemaphoreType.DMA((2 + SECTIONS,))] * 2,
         name="hand_on",
     )(*outs)
     return proj, hgrad.T, fgrad

time: 97.2 us -> 95.7 us (0.985)
  Pallas kernels: 96.5 us -> 95 us
    pallas_call x1, Pallas kernels: 93.8 us -> 92.6 us  [body(): pl.pallas_call(kernel, out_shape=(jax.ShapeDtypeStruct((ROWS, COL), BF16)...]
where the time goes in v6:
time: 95.7 us; the launch traced here: 95.6 us
  Pallas kernels  95 us (99%)
    pallas_call x1, Pallas kernels, body(): pl.pallas_call(kernel, out_shape=(jax.ShapeDtypeStruct((ROWS, COL), BF16)...  92.6 us
    pallas_call x1, Pallas kernels, body(): pl.pallas_call(hand_on, out_shape=tuple((jax.ShapeDtypeStruct(o.shape, o....  2.33 us

profile of v6, /device:TPU:1, one launch (start us, length us, event | category | flops | bytes accessed | tf_op | source)
XLA Modules:
  0.0 95.6 jit_solution(4654537561954198542)
XLA Ops:
  0.6 92.6 %butterfly.1 = (bf16[256,128]{1,0:T(8,128)(2,1)}, bf16[448,256]{1,0:T(8,128)(2,1)}, f32[6,7,64,64]{3,2,1,0:T(8,128)}) custom-call(bf16[448,256]{1,0:T(8,128)(2,1)} %bitcast.2, bf16[448,8192]{1,0:T(8,128)(2,1)} %w_hbm.1, bf16[6,7,64,64]{3,2,1,0:T(8,128)(2,1)} %fac_hbm.1, bf16[256,128]{1,0:T(8,128)(2,1)} %cot_hbm.1), custom_call_target="tpu_custom_call" | custom-call | tf_op jit(solution)/shard_map/butterfly/pallas_call | solution.py:543
  93.3 2.3 %hand_on.1 = (bf16[256,128]{1,0:T(8,128)(2,1)}, bf16[448,256]{1,0:T(8,128)(2,1)}, f32[6,7,64,64]{3,2,1,0:T(8,128)}) custom-call(bf16[256,128]{1,0:T(8,128)(2,1)} %get-tuple-element.9.proj, bf16[448,256]{1,0:T(8,128)(2,1)} %get-tuple-element.10.hgrad, f32[6,7,64,64]{3,2,1,0:T(8,128)} %get-tuple-element.11.fgrad), custom_call_target="tpu_custom_call" | custom-call | tf_op jit(solution)/shard_map/hand_on/pallas_call | solution.py:566

commit v7 on v6

--- a/solution.py
+++ b/solution.py
@@ -107,6 +107,19 @@
         started.append(c)
         return c
 
+    peers = [f(k) for f in (z_dev, x_dev, y_dev) for k in (1, 2, 3)]
+    run = lax.div(dp, 2) * SIDE + z
+
+    def run_dev(k):
+        to = lax.rem(run + k, 2 * SIDE)
+        return (lax.div(to, SIDE) * 2 + core, t - z + lax.rem(to, SIDE))
+
+    ends = [run_dev(1), run_dev(2 * SIDE - 1)]
+    peers += [core_dev] + ends
+    barrier = pltpu.get_barrier_semaphore()
+    for dev in peers:
+        pl.semaphore_signal(barrier, inc=1, device_id=dev, device_id_type=MESH)
+
     def fetch(src, dst, k):
         c = pltpu.make_async_copy(src, dst, in_sem.at[k])
         c.start()
@@ -125,18 +138,6 @@
         c.start()
         stored.append(c)
 
-    peers = [f(k) for f in (z_dev, x_dev, y_dev) for k in (1, 2, 3)]
-    run = lax.div(dp, 2) * SIDE + z
-
-    def run_dev(k):
-        to = lax.rem(run + k, 2 * SIDE)
-        return (lax.div(to, SIDE) * 2 + core, t - z + lax.rem(to, SIDE))
-
-    ends = [run_dev(1), run_dev(2 * SIDE - 1)]
-    peers += [core_dev] + ends
-    barrier = pltpu.get_barrier_semaphore()
-    for dev in peers:
-        pl.semaphore_signal(barrier, inc=1, device_id=dev, device_id_type=MESH)
     diag = (
         lax.broadcasted_iota(jnp.int32, (COL, WIDTH), 0) // HALF
         == lax.rem(lax.broadcasted_iota(jnp.int32, (COL, WIDTH), 1), COL) // HALF

time: 95.7 us -> 97.1 us (1.015)
  Pallas kernels: 95 us -> 96.4 us
    pallas_call x1, Pallas kernels: 92.6 us -> 94 us  [body(): pl.pallas_call(kernel, out_shape=(jax.ShapeDtypeStruct((ROWS, COL), BF16)...]
where the time goes in v7:
time: 97.1 us; the launch traced here: 97 us
  Pallas kernels  96.4 us (99%)
    pallas_call x1, Pallas kernels, body(): pl.pallas_call(kernel, out_shape=(jax.ShapeDtypeStruct((ROWS, COL), BF16)...  94 us
    pallas_call x1, Pallas kernels, body(): pl.pallas_call(hand_on, out_shape=tuple((jax.ShapeDtypeStruct(o.shape, o....  2.33 us

profile of v7, /device:TPU:1, one launch (start us, length us, event | category | flops | bytes accessed | tf_op | source)
XLA Modules:
  0.0 97.0 jit_solution(17612336421111355397)
XLA Ops:
  0.6 94.0 %butterfly.1 = (bf16[256,128]{1,0:T(8,128)(2,1)}, bf16[448,256]{1,0:T(8,128)(2,1)}, f32[6,7,64,64]{3,2,1,0:T(8,128)}) custom-call(bf16[448,256]{1,0:T(8,128)(2,1)} %bitcast.2, bf16[448,8192]{1,0:T(8,128)(2,1)} %w_hbm.1, bf16[6,7,64,64]{3,2,1,0:T(8,128)(2,1)} %fac_hbm.1, bf16[256,128]{1,0:T(8,128)(2,1)} %cot_hbm.1), custom_call_target="tpu_custom_call" | custom-call | tf_op jit(solution)/shard_map/butterfly/pallas_call | solution.py:544
  94.7 2.3 %hand_on.1 = (bf16[256,128]{1,0:T(8,128)(2,1)}, bf16[448,256]{1,0:T(8,128)(2,1)}, f32[6,7,64,64]{3,2,1,0:T(8,128)}) custom-call(bf16[256,128]{1,0:T(8,128)(2,1)} %get-tuple-element.9.proj, bf16[448,256]{1,0:T(8,128)(2,1)} %get-tuple-element.10.hgrad, f32[6,7,64,64]{3,2,1,0:T(8,128)} %get-tuple-element.11.fgrad), custom_call_target="tpu_custom_call" | custom-call | tf_op jit(solution)/shard_map/hand_on/pallas_call | solution.py:567
